TPU v7x, 256 devices: a whole 4x4x8 slice. The times are simulated.
256 devices in a mesh: gx: 8 (over z), gy: 4 (over y_lo, core), gz: 8 (over y_hi, x).
Axes of the slice: x: 4, y: 4 (y_hi: 2, y_lo: 2; y = y_hi * 2 + y_lo), z: 8, core: 2. Of those that a mesh axis runs over, the one named last changes fastest.
Arguments:
- positions: float32 [3, 8, 4, 8, 32], P(None, 'gx', 'gy', 'gz'), may hold values from 0 to 32, as said below
- features: float32 [8, 4, 8, 32, 256], P('gx', 'gy', 'gz'), may hold values from -6 to 6
- plane_send: int32 [8, 4, 8, 2, 2, 8], P('gx', 'gy', 'gz'), may hold values from 0 to 31
- vertical_send: int32 [8, 4, 8, 2, 8], P('gx', 'gy', 'gz'), may hold values from 0 to 159, as said below
- neighbours: int32 [8, 4, 8, 32, 48], P('gx', 'gy', 'gz'), may hold values from 0 to 191, as said below
- counts: int32 [8, 4, 8, 32], P('gx', 'gy', 'gz'), may hold values from 1 to 48, as said below
- query_weight: float32 [2, 256, 256], replicated, may hold values from -0.375 to 0.375
- key_weight: float32 [2, 256, 256], replicated, may hold values from -0.375 to 0.375
- radial_weight: float32 [2, 8, 256], replicated, may hold values from -2 to 2
- mix_weight: bfloat16 [2, 256, 256], replicated, may hold values from -0.375 to 0.375
- vector_weight: bfloat16 [2, 256, 64], replicated, may hold values from -0.375 to 0.375
- head_weight: float32 [256, 256], replicated, may hold values from -0.375 to 0.375
- energy_weight: float32 [256], replicated, may hold values from -0.375 to 0.375
Outputs:
- energies: float32 [8, 4, 8, 32], P('gx', 'gy', 'gz')
- forces: float32 [3, 8, 4, 8, 32], P(None, 'gx', 'gy', 'gz')
- feature_grad: float32 [8, 4, 8, 32, 256], P('gx', 'gy', 'gz')
Inputs may be any that keep to these rules, and one draw needn't show every extreme that they name: `vertical_send`: an own row, or a row of a plane cell that a neighbouring domain fills; never one of the four central cells, never a cell beyond the grid. `neighbours`: an own row other than the atom itself, a plane row as for vertical_send, or a row of z-cells 2 iz - 1 and 2 iz + 2. `counts`: every domain has an atom with all 48 slots live. `positions`: component 0 of domain (ix, iy, iz)'s atoms lies within 4 ix to 4 ix + 4, components 1 and 2 likewise with iy and iz.
All inputs are finite; a program needn't handle non-finite values.
Results may differ from a plain program's by a relative error of at most 0.011.
Values sent between devices are 32-bit elements; how exact they have to be, the bound alone decides.
A program may use at most 64 MiB of HBM per device.

v0:
```python
import math

import jax
import jax.numpy as jnp
from jax import lax
from jax.experimental import pallas as pl
from jax.experimental.pallas import tpu as pltpu
from jax.sharding import PartitionSpec as P

A, S, C, CT, NB, G = 32, 48, 256, 64, 8, 8
LAYERS = 2
EDGES = A * S
STEP = 256
CHUNKS = EDGES // STEP
CUTOFF, SOFTEN, BOX_SIDE = 6.0, 0.25, 4.0
FACTOR = 1.0 / math.sqrt(S)
F32, BF = jnp.float32, jnp.bfloat16

MESSAGES = (
    (1, 0, ((1, 0), (1, 1))),
    (-1, 0, ((0, 0), (0, 1))),
    (0, 1, ((0, 1), (1, 1))),
    (0, -1, ((0, 0), (1, 0))),
    (1, 1, ((1, 1),)),
    (1, -1, ((1, 0),)),
    (-1, 1, ((0, 1),)),
    (-1, -1, ((0, 0),)),
)
BLOCKS = tuple((dx, dy, a, b) for dx, dy, quads in MESSAGES for a, b in quads)
PLANE = G * len(BLOCKS)
FIRST = A + PLANE
ROWS = FIRST + 2 * G
LABELS = tuple(range(0, A, G)) + tuple(
    A + ((1 - 2 * dx + a) * 4 + 1 - 2 * dy + b) * G for dx, dy, a, b in BLOCKS
) + (A + 16 * G, A + 19 * G)
SELF = ROWS + A
DEPTH = 256


def mm(a, b):
    return lax.dot_general(a, b, (((1,), (0,)), ((), ())), preferred_element_type=F32)


def mm_nt(a, b):
    return lax.dot_general(a, b, (((1,), (1,)), ((), ())), preferred_element_type=F32)


def split(x):
    hi = x.astype(BF)
    return hi, (x - hi.astype(F32)).astype(BF)


def split3(x):
    hi, rest = x.astype(BF), x - x.astype(BF).astype(F32)
    mid = rest.astype(BF)
    return hi, mid, (rest - mid.astype(F32)).astype(BF)


def exact(product, a, b):
    ah, al = split(a)
    bh, bl = split(b)
    return product(ah, bh) + (product(ah, bl) + product(al, bh))


def iota(shape, dim):
    return lax.broadcasted_iota(jnp.int32, shape, dim)


def kernel(
    pos, feat, ps, vs, nbr, cnt, wr, we, wq_in, wk_in, wm_in, wv_in, wh_in,
    en_out, force_out, grad_out,
    wq, wk, wm, wv, wh,
    key_tab, key_send, face_send, pos_tab, pos_send, pos_face,
    dkey, key_back, key_ret, key_mine, dpos, pos_back, pos_ret, pos_mine,
    edge, weight, act, slope, dlat, mt, basis_s, dbasis_s, dw, db, dr_s,
    load_sem, send_sem, recv_sem,
):
    ix, iy, iz = (lax.axis_index(n) for n in ("gx", "gy", "gz"))
    nx, ny, nz = (lax.axis_size(n) for n in ("gx", "gy", "gz"))

    def at(dx, dy, dz):
        return {
            "gx": lax.rem(ix + (dx + nx), nx),
            "gy": lax.rem(iy + (dy + ny), ny),
            "gz": lax.rem(iz + (dz + nz), nz),
        }

    loads = {}
    for n, (name, src, dst) in enumerate(
        (
            ("wk", wk_in, wk),
            ("wq", wq_in, wq),
            ("wm", wm_in, wm),
            ("wv", wv_in, wv),
            ("wh", wh_in, wh),
        )
    ):
        loads[name] = pltpu.make_async_copy(src, dst, load_sem.at[n])
        loads[name].start()

    barrier = pltpu.get_barrier_semaphore()
    around = [(dx, dy, 0) for dx, dy, _ in MESSAGES] + [(0, 0, -1), (0, 0, 1)]
    for step in around:
        pl.semaphore_signal(barrier, inc=1, device_id=at(*step), device_id_type=pl.DeviceIdType.MESH)

    def remote(stage, src, dst, where):
        pltpu.make_async_remote_copy(
            src_ref=src,
            dst_ref=dst,
            send_sem=send_sem.at[stage],
            recv_sem=recv_sem.at[stage],
            device_id=where,
            device_id_type=pl.DeviceIdType.MESH,
        ).start()

    def plane(stage, src, src_at, dst, dst_at, sign):
        row = 0
        for dx, dy, quads in MESSAGES:
            rows = G * len(quads)
            remote(
                stage,
                src.at[pl.ds(src_at + row, rows)],
                dst.at[pl.ds(dst_at + row, rows)],
                at(sign * dx, sign * dy, 0),
            )
            row += rows

    def zone(stage, src, src_at, dst, dst_at):
        remote(stage, src.at[pl.ds(src_at, G)], dst.at[pl.ds(dst_at + G, G)], at(0, 0, -1))
        remote(stage, src.at[pl.ds(src_at + G, G)], dst.at[pl.ds(dst_at, G)], at(0, 0, 1))

    def arrived(stage, buf, row, rows):
        part = buf.at[pl.ds(row, rows)]
        pltpu.make_async_copy(part, part, recv_sem.at[stage]).wait()

    def sent(stage, buf, row, rows):
        part = buf.at[pl.ds(row, rows)]
        pltpu.make_async_copy(part, part, send_sem.at[stage]).wait()

    sub8, lane8 = iota((G, G), 0), iota((G, G), 1)

    def column(row):
        return jnp.sum(jnp.where(sub8 == lane8, row.astype(F32), 0.0), axis=1, keepdims=True)

    quads = [column(ps[q : q + 1, :]) for q in range(4)]
    lane32 = iota((G, A), 1).astype(F32)
    picks = [jnp.where(quads[2 * a + b] == lane32, 1.0, 0.0) for _, _, a, b in BLOCKS]
    eye = jnp.where(iota((A, A), 0) == iota((A, A), 1), 1.0, 0.0)
    pick_f = jnp.concatenate([eye] + picks, axis=0)
    pick = pick_f.astype(BF)

    own_parts = split3(pos[...])

    def place_rows(part):
        wide = jnp.concatenate([part.astype(F32), jnp.zeros((128 - 3, A), F32)], axis=0)
        return mm_nt(pick, wide.astype(BF))

    place = place_rows(own_parts[0]) + place_rows(own_parts[1]) + place_rows(own_parts[2])
    pos_tab[pl.ds(0, A), :] = place[:A]
    pos_send[...] = place[A:]

    pl.semaphore_wait(barrier, len(around))
    plane(0, pos_send, 0, pos_tab, A, 1)

    loads["wk"].wait()
    h0 = feat[...]

    def send_keys(layer, h):
        keys = exact(mm, h, wk[layer])
        rows = mm(pick, keys.astype(BF))
        key_tab[layer, pl.ds(0, A), :] = rows[:A]
        key_send[layer] = rows[A:]
        plane(2 + 2 * layer, key_send.at[layer], 0, key_tab.at[layer], A, 1)

    send_keys(0, h0)

    lane_first = iota((1, FIRST), 1)
    label_row = lane_first
    for n in range(A // G, FIRST // G):
        label_row = label_row + jnp.where(lane_first // G == n, LABELS[n] - n * G, 0)
    label_row = label_row.astype(F32)
    face_f = jnp.concatenate(
        [jnp.where(column(vs[f : f + 1, :]) == label_row, 1.0, 0.0) for f in range(2)], axis=0
    )
    face = face_f.astype(BF)
    face_t = jnp.concatenate([face_f, face_f], axis=0).T.astype(BF)
    pick_q = pick_f[A:]
    pick_t = jnp.concatenate([pick_q, pick_q], axis=0).T.astype(BF)

    atom = iota((A, EDGES), 1) & (A - 1)
    mine = atom == iota((A, EDGES), 0)
    slot_pick = jnp.where((iota((S, EDGES), 1) >> 5) == iota((S, EDGES), 0), 1.0, 0.0).astype(BF)
    nbr_all = mm(nbr[...].astype(F32).astype(BF), slot_pick)
    nbr_row = jnp.sum(jnp.where(mine, nbr_all, 0.0), axis=0, keepdims=True)
    mine_f = jnp.where(mine, 1.0, 0.0)
    mine_b = mine_f.astype(BF)
    cnt_rows = jnp.broadcast_to(cnt[...].astype(F32), (16, A)).astype(BF)
    cnt_row = mm(cnt_rows, mine_b)[0:1]
    live = jnp.where((iota((1, EDGES), 1) >> 5).astype(F32) < cnt_row, 1.0, 0.0)
    tile = iota((16, EDGES), 0)
    for n in range(ROWS // 16):
        low, high = LABELS[2 * n], LABELS[2 * n + 1]
        label = jnp.where(tile < G, tile + low, tile + (high - G)).astype(F32)
        edge[pl.ds(16 * n, 16), :] = jnp.where(nbr_row == label, 1.0, 0.0).astype(BF)
    edge[pl.ds(ROWS, A), :] = mine_b
    edge[pl.ds(SELF, DEPTH - SELF), :] = jnp.zeros((DEPTH - SELF, EDGES), BF)
    dr_s[...] = jnp.zeros_like(dr_s)

    arrived(0, pos_tab, A, PLANE)
    first = pos_tab[pl.ds(0, FIRST), :]
    rows = sum(mm(face, part) for part in split3(first))
    span = BOX_SIDE * nz
    low_shift = jnp.where(iz == 0, span, 0.0).astype(F32)
    high_shift = jnp.where(iz == nz - 1, -span, 0.0).astype(F32)
    shift = jnp.where(iota((2 * G, 128), 0) < G, low_shift, high_shift)
    pos_face[...] = rows + jnp.where(iota((2 * G, 128), 1) == 2, shift, 0.0)
    zone(1, pos_face, 0, pos_tab, FIRST)

    def send_faces(layer):
        arrived(2 + 2 * layer, key_tab.at[layer], A, PLANE)
        first_keys = key_tab[layer, pl.ds(0, FIRST), :].astype(BF)
        face_send[layer] = mm(face, first_keys)
        zone(3 + 2 * layer, face_send.at[layer], 0, key_tab.at[layer], FIRST)

    send_faces(0)

    arrived(1, pos_tab, FIRST, 2 * G)
    place = jnp.concatenate([pos_tab[...], -pos_tab[pl.ds(0, A), :]], axis=0)
    place = jnp.concatenate([place, jnp.zeros((DEPTH - SELF, 128), F32)], axis=0)
    place_t = place.T[0:G, :]
    parts = [part.astype(F32) for part in split3(place_t)] + [jnp.zeros((G, DEPTH), F32)]
    offset = mm(jnp.concatenate(parts, axis=0).astype(BF), edge[...])
    offset = offset[0:G] + (offset[G : 2 * G] + offset[2 * G : 3 * G])
    dist2 = jnp.sum(offset * offset, axis=0, keepdims=True) + SOFTEN
    dist = jnp.sqrt(dist2)
    inv = 1.0 / dist
    scaled = dist * (1.0 / CUTOFF)
    gap = 1.0 - scaled * scaled
    inside = jnp.where(scaled < 1.0, live, 0.0)
    envelope = inside * gap * gap
    direction = offset * inv
    order = (iota((NB, EDGES), 0) + 1).astype(F32)
    turn = order * scaled
    whole = jnp.floor(turn + 0.5)
    angle = (turn - whole) * math.pi
    sign = 1.0 - 2.0 * (whole - 2.0 * jnp.floor(0.5 * whole))
    sq = angle * angle
    sine, cosine = jnp.zeros_like(sq), jnp.zeros_like(sq)
    for n in range(6, -1, -1):
        sine = sine * sq + (-1.0) ** n / math.factorial(2 * n + 1)
        cosine = cosine * sq + (-1.0) ** n / math.factorial(2 * n)
    inv_scaled = CUTOFF * inv
    basis = sign * sine * angle * inv_scaled
    basis_s[...] = basis
    dbasis_s[...] = (order * math.pi * sign * cosine - basis) * inv_scaled
    basis_h, basis_l = split(basis)
    basis_h, basis_l = basis_h.astype(F32), basis_l.astype(F32)
    edge[pl.ds(SELF, 32), :] = jnp.concatenate(
        [basis_h, basis_l, basis_h, jnp.zeros_like(basis)], axis=0
    ).astype(BF)
    for q in range(4):
        row = envelope if q == 0 else envelope * direction[q - 1 : q]
        w_h, w_l = split(row * mine_f)
        weight[pl.ds(A * q, A), :] = w_h
        weight[pl.ds(4 * A + A * q, A), :] = w_l

    def forward(layer, h, queries):
        radial = wr[layer]
        radial_h, radial_l = split(radial)
        radial_h, radial_l = radial_h.astype(F32), radial_l.astype(F32)
        arrived(3 + 2 * layer, key_tab.at[layer], FIRST, 2 * G)
        rows = jnp.concatenate(
            [
                key_tab[layer],
                queries,
                radial_h,
                radial_h,
                radial_l,
                jnp.zeros((DEPTH - SELF - 3 * NB, C), F32),
            ],
            axis=0,
        )
        mt[...] = rows.T.astype(BF)

        def step(n, carry):
            part = pl.ds(pl.multiple_of(n * STEP, STEP), STEP)
            latent = mm(mt[...], edge[:, part])
            gate = 0.5 * jnp.tanh(0.5 * latent) + 0.5
            active = latent * gate
            act[layer, :, part] = active.astype(BF)
            slope[layer, :, part] = gate + active * (1.0 - gate)
            return carry

        lax.fori_loop(0, CHUNKS, step, 0)
        total = mm_nt(weight[...], act[layer])
        total = total[: 4 * A] + total[4 * A :]
        gather_h, gather_l = split(total[:A])
        new = h + FACTOR * (mm(gather_h, wm[layer]) + mm(gather_l, wm[layer]))
        vec_h, vec_l = split(total[A:])
        vector = FACTOR * (mm(vec_h, wv[layer]) + mm(vec_l, wv[layer]))
        return new, vector

    loads["wq"].wait()
    q0 = exact(mm, h0, wq[0])
    loads["wm"].wait()
    loads["wv"].wait()
    h1, v0 = forward(0, h0, q0)
    send_keys(1, h1)
    q1 = exact(mm, h1, wq[1])
    send_faces(1)
    loads["wh"].wait()
    h2, v1 = forward(1, h1, q1)

    lat = exact(mm, h2, wh[...])
    gate = 0.5 * jnp.tanh(0.5 * lat) + 0.5
    hidden = lat * gate
    readout = we[...]
    square = v0 * v0 + v1 * v1
    square = square[:A] + (square[A : 2 * A] + square[2 * A :])
    energy = jnp.sum(hidden * readout, axis=1, keepdims=True) + jnp.sum(
        square, axis=1, keepdims=True
    ) * (1.0 / CT)
    en_out[...] = jnp.sum(eye * energy, axis=0, keepdims=True)
    dh2 = exact(mm_nt, readout * (gate + hidden * (1.0 - gate)), wh[...])

    chunk_mine = mine_f[:, :STEP]

    def backward(layer, dh, vector):
        dh_h, dh_l = split(dh)
        g0 = FACTOR * (mm_nt(dh_h, wm[layer]) + mm_nt(dh_l, wm[layer]))
        dv_h, dv_l = split(vector * (2.0 / CT))
        gx = FACTOR * (mm_nt(dv_h, wv[layer]) + mm_nt(dv_l, wv[layer]))
        pull = jnp.concatenate([g0, gx], axis=0)
        pull_b = pull.astype(BF)
        mt[...] = jnp.concatenate([pull, pull], axis=0).T.astype(BF)
        radial_h, radial_l = split(wr[layer])
        radial = jnp.concatenate([radial_h.astype(F32), radial_l.astype(F32)], axis=0).astype(BF)

        def step(n, carry):
            part = pl.ds(pl.multiple_of(n * STEP, STEP), STEP)
            dl = (mm(mt[...], weight[:, part]) * slope[layer, :, part]).astype(BF)
            dlat[:, part] = dl
            cross = mm(pull_b, act[layer, :, part])
            rows = [
                jnp.sum(cross[A * q : A * q + A] * chunk_mine, axis=0, keepdims=True)
                for q in range(4)
            ]
            rows = jnp.concatenate(rows + [jnp.zeros((4, STEP), F32)], axis=0)
            got = mm(radial, dl)
            got = got[:NB] + got[NB:]
            if layer == LAYERS - 1:
                dw[:, part] = rows
                db[:, part] = got
            else:
                dw[:, part] += rows
                db[:, part] += got
            return carry

        lax.fori_loop(0, CHUNKS, step, 0)
        drows = mm_nt(edge[pl.ds(0, SELF), :], dlat[...])
        dkey[layer] = drows[:ROWS]
        zone(6 + 2 * layer, dkey.at[layer], FIRST, key_back.at[layer], 0)
        return drows[ROWS:]

    def add_faces(first, back):
        back_h, back_l = split(back)
        return first + mm(face_t, jnp.concatenate([back_h, back_l], axis=0))

    def add_quads(own, back):
        back_h, back_l = split(back)
        return own + mm(pick_t, jnp.concatenate([back_h, back_l], axis=0))

    def return_planes(layer):
        arrived(6 + 2 * layer, key_back.at[layer], 0, 2 * G)
        total = add_faces(dkey[layer, pl.ds(0, FIRST), :], key_back[layer])
        key_ret[layer] = total[A:]
        plane(7 + 2 * layer, key_ret.at[layer], 0, key_mine.at[layer], 0, -1)
        return total[:A]

    def finish(layer, own, dh, dquery):
        arrived(7 + 2 * layer, key_mine.at[layer], 0, PLANE)
        own = add_quads(own, key_mine[layer])
        return dh + dquery + exact(mm_nt, own, wk[layer])

    dq1 = backward(1, dh2, v1)
    dq1 = exact(mm_nt, dq1, wq[1])
    own1 = return_planes(1)
    dh1 = finish(1, own1, dh2, dq1)
    dq0 = backward(0, dh1, v0)

    de = dw[0:1]
    unit = direction
    for q in range(3):
        de = de + dw[q + 1 : q + 2] * unit[q : q + 1]
    lanes = iota((G, EDGES), 0)
    du = jnp.zeros((G, EDGES), F32)
    for q in range(3):
        du = jnp.where(lanes == q, dw[q + 1 : q + 2], du)
    du = du * envelope
    dscaled = -4.0 * inside * gap * scaled * de + jnp.sum(
        db[...] * dbasis_s[...], axis=0, keepdims=True
    )
    ddist = dscaled * (1.0 / CUTOFF) - inv * jnp.sum(du * unit, axis=0, keepdims=True)
    dr_h, dr_l = split(du * inv + unit * ddist)
    dr_s[pl.ds(0, 16), :] = jnp.concatenate([dr_h.astype(F32), dr_l.astype(F32)], axis=0).astype(BF)
    rows = mm_nt(edge[pl.ds(0, SELF), :], dr_s[...])
    dpos[...] = rows[:ROWS]
    zone(10, dpos, FIRST, pos_back, 0)
    pos_own = rows[:A] - rows[ROWS:]

    own0 = return_planes(0)
    dq0 = exact(mm_nt, dq0, wq[0])
    arrived(10, pos_back, 0, 2 * G)
    total = add_faces(dpos[pl.ds(0, FIRST), :], pos_back[...])
    pos_ret[...] = total[A:]
    plane(11, pos_ret, 0, pos_mine, 0, -1)
    pos_own = total[:A] - rows[ROWS:]
    grad_out[...] = finish(0, own0, dh1, dq0)
    arrived(11, pos_mine, 0, PLANE)
    pos_own = add_quads(pos_own, pos_mine[...])
    pos_own = jnp.concatenate([pos_own, jnp.zeros((128 - A, 128), F32)], axis=0).T
    force_out[...] = -(pos_own[0:3, :A] + pos_own[G : G + 3, :A])

    sent(0, pos_send, 0, PLANE)
    sent(1, pos_face, 0, 2 * G)
    for layer in range(LAYERS):
        sent(2 + 2 * layer, key_send.at[layer], 0, PLANE)
        sent(3 + 2 * layer, face_send.at[layer], 0, 2 * G)
        sent(6 + 2 * layer, dkey.at[layer], FIRST, 2 * G)
        sent(7 + 2 * layer, key_ret.at[layer], 0, PLANE)
    sent(10, dpos, FIRST, 2 * G)
    sent(11, pos_ret, 0, PLANE)


def per_device(
    positions, features, plane_send, vertical_send, neighbours, counts,
    query_weight, key_weight, radial_weight, mix_weight, vector_weight, head_weight, energy_weight,
):
    vmem = pl.BlockSpec(memory_space=pltpu.VMEM)
    hbm = pl.BlockSpec(memory_space=pl.ANY)
    energies, forces, grad = pl.pallas_call(
        kernel,
        out_shape=(
            jax.ShapeDtypeStruct((1, A), F32),
            jax.ShapeDtypeStruct((3, A), F32),
            jax.ShapeDtypeStruct((A, C), F32),
        ),
        in_specs=[vmem] * 8 + [hbm] * 5,
        out_specs=(vmem,) * 3,
        scratch_shapes=[
            pltpu.VMEM((LAYERS, C, C), F32),
            pltpu.VMEM((LAYERS, C, C), F32),
            pltpu.VMEM((LAYERS, C, C), BF),
            pltpu.VMEM((LAYERS, C, CT), BF),
            pltpu.VMEM((C, C), F32),
            pltpu.VMEM((LAYERS, ROWS, C), F32),
            pltpu.VMEM((LAYERS, PLANE, C), F32),
            pltpu.VMEM((LAYERS, 2 * G, C), F32),
            pltpu.VMEM((ROWS, 128), F32),
            pltpu.VMEM((PLANE, 128), F32),
            pltpu.VMEM((2 * G, 128), F32),
            pltpu.VMEM((LAYERS, ROWS, C), F32),
            pltpu.VMEM((LAYERS, 2 * G, C), F32),
            pltpu.VMEM((LAYERS, PLANE, C), F32),
            pltpu.VMEM((LAYERS, PLANE, C), F32),
            pltpu.VMEM((ROWS, 128), F32),
            pltpu.VMEM((2 * G, 128), F32),
            pltpu.VMEM((PLANE, 128), F32),
            pltpu.VMEM((PLANE, 128), F32),
            pltpu.VMEM((DEPTH, EDGES), BF),
            pltpu.VMEM((8 * A, EDGES), BF),
            pltpu.VMEM((LAYERS, C, EDGES), BF),
            pltpu.VMEM((LAYERS, C, EDGES), F32),
            pltpu.VMEM((C, EDGES), BF),
            pltpu.VMEM((C, C), BF),
            pltpu.VMEM((NB, EDGES), F32),
            pltpu.VMEM((NB, EDGES), F32),
            pltpu.VMEM((8, EDGES), F32),
            pltpu.VMEM((NB, EDGES), F32),
            pltpu.VMEM((128, EDGES), BF),
            pltpu.SemaphoreType.DMA((5,)),
            pltpu.SemaphoreType.DMA((12,)),
            pltpu.SemaphoreType.DMA((12,)),
        ],
        compiler_params=pltpu.CompilerParams(
            collective_id=0, has_side_effects=True, vmem_limit_bytes=32 * 1024 * 1024
        ),
        cost_estimate=pl.CostEstimate(
            flops=2_500_000_000, bytes_accessed=2_000_000, transcendentals=800_000
        ),
    )(
        positions.reshape(3, A),
        features.reshape(A, C),
        plane_send.reshape(4, G),
        vertical_send.reshape(2, G),
        neighbours.reshape(A, S),
        counts.reshape(1, A),
        radial_weight,
        energy_weight.reshape(1, C),
        query_weight,
        key_weight,
        mix_weight,
        vector_weight,
        head_weight,
    )
    return (
        energies.reshape(1, 1, 1, A),
        forces.reshape(3, 1, 1, 1, A),
        grad.reshape(1, 1, 1, A, C),
    )


def solution(mesh):
    return jax.shard_map(
        per_device,
        mesh=mesh,
        in_specs=(
            P(None, "gx", "gy", "gz", None),
            P("gx", "gy", "gz", None, None),
            P("gx", "gy", "gz", None, None, None),
            P("gx", "gy", "gz", None, None),
            P("gx", "gy", "gz", None, None),
            P("gx", "gy", "gz", None),
            P(),
            P(),
            P(),
            P(),
            P(),
            P(),
            P(),
        ),
        out_specs=(
            P("gx", "gy", "gz", None),
            P(None, "gx", "gy", "gz", None),
            P("gx", "gy", "gz", None, None),
        ),
        check_vma=False,
    )
```

profile of v0, /device:TPU:1, one launch (start us, length us, event | category | flops | bytes accessed | tf_op | source)
XLA Modules:
  0.0 63.7 jit_solution(1573087442195256110)
XLA Ops:
  0.6 0.0 copy-start.11
  0.6 0.7 %copy-done.11 = f32[3,1,1,1,32]{4,3,2,1,0:T(1,128)S(1)} copy-done((f32[3,1,1,1,32]{4,3,2,1,0:T(1,128)S(1)}, f32[3,1,1,1,32]{4,3,2,1,0:T(1,128)}, u32[]{:S(2)}) %copy-start.11) | copy-done | bytes 408
  1.3 0.0 copy-start.4
  1.3 0.0 copy-start.5
  1.3 0.0 copy-start.6
  1.3 0.0 copy-start.7
  1.3 0.0 copy-start.8
  1.3 0.0 copy-start.9
  1.4 0.0 copy-start.10
  1.4 1.0 %copy.16.wv_in = bf16[2,256,64]{2,1,0:T(8,128)(2,1)S(1)} copy(bf16[2,256,64]{1,2,0:T(8,128)(2,1)} %param.23) | data formatting | bytes 131072 | tf_op args[10]
  2.4 0.0 copy-done.4
  2.4 0.0 copy-done.5
  2.4 0.0 copy-done.6
  2.4 0.0 copy-done.7
  2.4 0.0 copy-done.8
  2.4 0.0 copy-done.9
  2.4 0.0 copy-done.10
  2.5 0.0 copy-start
  2.5 1.0 %copy-done = f32[2,256,256]{2,1,0:T(8,128)S(1)} copy-done((f32[2,256,256]{2,1,0:T(8,128)S(1)}, f32[2,256,256]{2,1,0:T(8,128)}, u32[]{:S(2)}) %copy-start) | copy-done | bytes 524312
  3.5 0.0 copy-start.1
  3.5 1.0 %copy-done.1 = f32[2,256,256]{2,1,0:T(8,128)S(1)} copy-done((f32[2,256,256]{2,1,0:T(8,128)S(1)}, f32[2,256,256]{2,1,0:T(8,128)}, u32[]{:S(2)}) %copy-start.1) | copy-done | bytes 524312
  4.5 0.0 copy-start.2
  4.5 0.9 %copy-done.2 = bf16[2,256,256]{2,1,0:T(8,128)(2,1)S(1)} copy-done((bf16[2,256,256]{2,1,0:T(8,128)(2,1)S(1)}, bf16[2,256,256]{2,1,0:T(8,128)(2,1)}, u32[]{:S(2)}) %copy-start.2) | copy-done | bytes 262168
  5.5 0.0 copy-start.3
  5.5 0.9 %copy-done.3 = f32[256,256]{1,0:T(8,128)S(1)} copy-done((f32[256,256]{1,0:T(8,128)S(1)}, f32[256,256]{1,0:T(8,128)}, u32[]{:S(2)}) %copy-start.3) | copy-done | bytes 262168
  6.4 55.6 %shard_map.148 = (f32[1,32]{1,0:T(1,128)S(1)}, f32[3,32]{1,0:T(4,128)S(1)}, f32[32,256]{1,0:T(8,128)S(1)}) custom-call(f32[3,32]{1,0:T(4,128)S(1)} %bitcast.14, f32[32,256]{1,0:T(8,128)S(1)} %bitcast.15, s32[4,8]{1,0:T(4,128)S(1)} %bitcast.17, s32[2,8]{1,0:T(2,128)S(1)} %bitcast.18, s32[32,48]{1,0:T(8,128)S(1)} %bitcast.16, s32[1,32]{1,0:T(1,128)S(1)} %bitcast.20, ...), custom_call_target="tpu_custom_call" | custom-call | flops 2500000000 | bytes 2000000 | tf_op jit(solution)/shard_map/pallas_call | solution.py:441
  62.0 0.6 copy.17
  62.6 0.5 copy.23
  63.1 0.6 copy.24
  (1 shorter events, 0.0 us)
Async XLA Ops:
  0.6 0.7 %copy-start.11 = (f32[3,1,1,1,32]{4,3,2,1,0:T(1,128)S(1)}, f32[3,1,1,1,32]{4,3,2,1,0:T(1,128)}, u32[]{:S(2)}) copy-start(f32[3,1,1,1,32]{4,3,2,1,0:T(1,128)} %param.13) | copy-start | bytes 1156
  1.3 1.1 %copy-start.4 = (f32[1,1,1,32,256]{4,3,2,1,0:T(8,128)S(1)}, f32[1,1,1,32,256]{4,3,2,1,0:T(8,128)}, u32[]{:S(2)}) copy-start(f32[1,1,1,32,256]{4,3,2,1,0:T(8,128)} %param.14) | copy-start | bytes 98308
  1.3 1.1 %copy-start.5 = (s32[1,1,1,32,48]{4,3,2,1,0:T(8,128)S(1)}, s32[1,1,1,32,48]{4,3,2,1,0:T(8,128)}, u32[]{:S(2)}) copy-start(s32[1,1,1,32,48]{4,3,2,1,0:T(8,128)} %param.17) | copy-start | bytes 18436
  1.3 1.1 %copy-start.6 = (f32[2,8,256]{2,1,0:T(8,128)S(1)}, f32[2,8,256]{2,1,0:T(8,128)}, u32[]{:S(2)}) copy-start(f32[2,8,256]{2,1,0:T(8,128)} %wr.1) | copy-start | bytes 49156
  1.3 1.1 %copy-start.7 = (s32[1,1,1,2,2,8]{5,4,3,2,1,0:T(2,128)S(1)}, s32[1,1,1,2,2,8]{5,4,3,2,1,0:T(2,128)}, u32[]{:S(2)}) copy-start(s32[1,1,1,2,2,8]{5,4,3,2,1,0:T(2,128)} %param.15) | copy-start | bytes 388
  1.3 1.1 %copy-start.8 = (s32[1,1,1,2,8]{4,3,2,1,0:T(2,128)S(1)}, s32[1,1,1,2,8]{4,3,2,1,0:T(2,128)}, u32[]{:S(2)}) copy-start(s32[1,1,1,2,8]{4,3,2,1,0:T(2,128)} %param.16) | copy-start | bytes 196
  1.3 1.1 %copy-start.9 = (f32[256]{0:T(256)S(1)}, f32[256]{0:T(256)}, u32[]{:S(2)}) copy-start(f32[256]{0:T(256)} %param.25) | copy-start | bytes 3076
  1.4 1.1 %copy-start.10 = (s32[1,1,1,32]{3,2,1,0:T(1,128)S(1)}, s32[1,1,1,32]{3,2,1,0:T(1,128)}, u32[]{:S(2)}) copy-start(s32[1,1,1,32]{3,2,1,0:T(1,128)} %param.18) | copy-start | bytes 388
  2.5 1.0 %copy-start = (f32[2,256,256]{2,1,0:T(8,128)S(1)}, f32[2,256,256]{2,1,0:T(8,128)}, u32[]{:S(2)}) copy-start(f32[2,256,256]{2,1,0:T(8,128)} %wq_in.1) | copy-start | bytes 1572868
  3.5 1.0 %copy-start.1 = (f32[2,256,256]{2,1,0:T(8,128)S(1)}, f32[2,256,256]{2,1,0:T(8,128)}, u32[]{:S(2)}) copy-start(f32[2,256,256]{2,1,0:T(8,128)} %wk_in.1) | copy-start | bytes 1572868
  4.5 0.9 %copy-start.2 = (bf16[2,256,256]{2,1,0:T(8,128)(2,1)S(1)}, bf16[2,256,256]{2,1,0:T(8,128)(2,1)}, u32[]{:S(2)}) copy-start(bf16[2,256,256]{2,1,0:T(8,128)(2,1)} %wm_in.1) | copy-start | bytes 786436
  5.5 0.9 %copy-start.3 = (f32[256,256]{1,0:T(8,128)S(1)}, f32[256,256]{1,0:T(8,128)}, u32[]{:S(2)}) copy-start(f32[256,256]{1,0:T(8,128)} %wh_in.1) | copy-start | bytes 786436
where the time goes:
time: 64 us; the launch traced here: 63.7 us
  Pallas kernels  55.6 us (87%)
  local copies, waits for them, and re-layouts  7.39 us (12%)
  between operations  0.76 us (1%)
    pallas_call x1, Pallas kernels, per_device(): pl.pallas_call(kernel, out_shape=(jax.ShapeDtypeStruct((1, A), F32), jax....  55.6 us
    unnamed x29, local copies, waits for them, and re-layouts  7.39 us

commit v1 on v0

v1 whole, which is shorter than its diff:
```python
import math

import jax
import jax.numpy as jnp
from jax import lax
from jax.experimental import pallas as pl
from jax.experimental.pallas import tpu as pltpu
from jax.sharding import PartitionSpec as P

A, S, C, CT, NB, G = 32, 48, 256, 64, 8, 8
LAYERS = 2
EDGES = A * S
STEP = 256
CHUNKS = EDGES // STEP
CUTOFF, SOFTEN, BOX_SIDE = 6.0, 0.25, 4.0
FACTOR = 1.0 / math.sqrt(S)
F32, BF = jnp.float32, jnp.bfloat16

MESSAGES = (
    (1, 0, ((1, 0), (1, 1))),
    (-1, 0, ((0, 0), (0, 1))),
    (0, 1, ((0, 1), (1, 1))),
    (0, -1, ((0, 0), (1, 0))),
    (1, 1, ((1, 1),)),
    (1, -1, ((1, 0),)),
    (-1, 1, ((0, 1),)),
    (-1, -1, ((0, 0),)),
)
BLOCKS = tuple((dx, dy, a, b) for dx, dy, quads in MESSAGES for a, b in quads)
PLANE = G * len(BLOCKS)
FIRST = A + PLANE
ROWS = FIRST + 2 * G
LABELS = tuple(range(0, A, G)) + tuple(
    A + ((1 - 2 * dx + a) * 4 + 1 - 2 * dy + b) * G for dx, dy, a, b in BLOCKS
) + (A + 16 * G, A + 19 * G)
SELF = ROWS + A
DEPTH = 256
PLACES = tuple((dx, dy) for dx, dy, _ in MESSAGES) + ((0, 0),)
ZONE = 2 * G * len(PLACES)
BACK = PLANE + ZONE


def mm(a, b):
    return lax.dot_general(a, b, (((1,), (0,)), ((), ())), preferred_element_type=F32)


def mm_nt(a, b):
    return lax.dot_general(a, b, (((1,), (1,)), ((), ())), preferred_element_type=F32)


def split(x):
    hi = x.astype(BF)
    return hi, (x - hi.astype(F32)).astype(BF)


def split3(x):
    hi, rest = x.astype(BF), x - x.astype(BF).astype(F32)
    mid = rest.astype(BF)
    return hi, mid, (rest - mid.astype(F32)).astype(BF)


def exact(product, a, b):
    ah, al = split(a)
    bh, bl = split(b)
    return product(ah, bh) + (product(ah, bl) + product(al, bh))


def iota(shape, dim):
    return lax.broadcasted_iota(jnp.int32, shape, dim)


def kernel(
    pos_in, feat_in, ps_in, vs_in, nbr_in, cnt_in, wq_in, wk_in, wr_in, wm_in, wv_in, wh_in, we_in,
    en_out, force_out, grad_out,
    pos, feat, ps, vs, nbr, cnt, wq, wk, wr, wm, wv, wh, we,
    face_mine, face_all, pos_tab, pos_send, pos_face, pos_grad, pos_back,
    key_tab, key_send, face_send, zone_in, dkey, key_back,
    pick_all, pick_back, mine_s, geo, unit_s, dbasis_s, edge, weight, act, slope, dlat,
    mt, mp, dw, db, dr_s, h1_s, h2_s, dh_s, dq_s, own_s, query_s, vec_s,
    load_sem, send_sem, recv_sem,
):
    ix, iy, iz = (lax.axis_index(n) for n in ("gx", "gy", "gz"))
    nx, ny, nz = (lax.axis_size(n) for n in ("gx", "gy", "gz"))

    def at(dx, dy, dz):
        return {
            "gx": lax.rem(ix + (dx + nx), nx),
            "gy": lax.rem(iy + (dy + ny), ny),
            "gz": lax.rem(iz + (dz + nz), nz),
        }

    loads = {}
    for n, (name, src, dst) in enumerate(
        (
            ("ps", ps_in, ps),
            ("pos", pos_in, pos),
            ("feat", feat_in, feat),
            ("wk", wk_in, wk),
            ("vs", vs_in, vs),
            ("nbr", nbr_in, nbr),
            ("cnt", cnt_in, cnt),
            ("wr", wr_in, wr),
            ("wq", wq_in, wq),
            ("wm", wm_in, wm),
            ("wv", wv_in, wv),
            ("wh", wh_in, wh),
            ("we", we_in, we),
        )
    ):
        loads[name] = pltpu.make_async_copy(src, dst, load_sem.at[n])
        loads[name].start()

    barrier = pltpu.get_barrier_semaphore()
    around = [(dx, dy, 0) for dx, dy, _ in MESSAGES] + [(0, 0, -1), (0, 0, 1)]
    for step in around:
        pl.semaphore_signal(barrier, inc=1, device_id=at(*step), device_id_type=pl.DeviceIdType.MESH)

    def remote(stage, src, dst, where):
        pltpu.make_async_remote_copy(
            src_ref=src,
            dst_ref=dst,
            send_sem=send_sem.at[stage],
            recv_sem=recv_sem.at[stage],
            device_id=where,
            device_id_type=pl.DeviceIdType.MESH,
        ).start()

    def plane(stage, src, src_at, dst, dst_at, sign):
        row = 0
        for dx, dy, quads in MESSAGES:
            rows = G * len(quads)
            remote(
                stage,
                src.at[pl.ds(src_at + row, rows)],
                dst.at[pl.ds(dst_at + row, rows)],
                at(sign * dx, sign * dy, 0),
            )
            row += rows

    def zone(stage, src, src_at, dst, dst_at):
        remote(stage, src.at[pl.ds(src_at, G)], dst.at[pl.ds(dst_at + G, G)], at(0, 0, -1))
        remote(stage, src.at[pl.ds(src_at + G, G)], dst.at[pl.ds(dst_at, G)], at(0, 0, 1))

    def zone_out(stage, src, src_at, dst):
        for m, (dx, dy) in enumerate(PLACES):
            for f, dz in ((0, -1), (1, 1)):
                remote(
                    stage,
                    src.at[pl.ds(src_at + (2 * m + f) * G, G)],
                    dst.at[pl.ds((2 * m + 1 - f) * G, G)],
                    at(-dx, -dy, dz),
                )

    def give_back(stage, src, dst):
        for m, (dx, dy) in enumerate(PLACES):
            for b, dz in ((0, -1), (1, 1)):
                remote(
                    stage,
                    src.at[pl.ds(FIRST + b * G, G)],
                    dst.at[pl.ds(PLANE + (2 * m + 1 - b) * G, G)],
                    at(dx, dy, dz),
                )
        plane(stage, src, A, dst, 0, -1)

    def arrived(stage, buf, row, rows):
        part = buf.at[pl.ds(row, rows)]

        @pl.when(ix >= 0)
        def _():
            pltpu.make_async_copy(part, part, recv_sem.at[stage]).wait()

    def sent(stage, buf, row, rows):
        part = buf.at[pl.ds(row, rows)]
        pltpu.make_async_copy(part, part, send_sem.at[stage]).wait()

    sub8, lane8 = iota((G, G), 0), iota((G, G), 1)

    def column(row):
        return jnp.sum(jnp.where(sub8 == lane8, row.astype(F32), 0.0), axis=1, keepdims=True)

    loads["ps"].wait()
    lane32 = iota((G, A), 1).astype(F32)
    quads = {
        (a, b): jnp.where(column(ps[0, 0, 0, a, b : b + 1, :]) == lane32, 1.0, 0.0)
        for a in range(2)
        for b in range(2)
    }
    eye = jnp.where(iota((A, A), 0) == iota((A, A), 1), 1.0, 0.0)
    pick_f = jnp.concatenate([eye] + [quads[a, b] for _, _, a, b in BLOCKS], axis=0)
    pick = pick_f.astype(BF)
    pick_all[pl.ds(0, FIRST), :] = pick

    loads["pos"].wait()
    own_parts = split3(jnp.concatenate([pos[q, 0, 0] for q in range(3)], axis=0))

    def place_rows(part):
        wide = jnp.concatenate([part.astype(F32), jnp.zeros((128 - 3, A), F32)], axis=0)
        return mm_nt(pick, wide.astype(BF))

    place = place_rows(own_parts[0]) + place_rows(own_parts[1]) + place_rows(own_parts[2])
    pos_tab[pl.ds(0, A), :] = place[:A]
    pos_send[...] = place[A:]

    def own_keys(layer, h):
        return exact(mm, h, wk[layer]).astype(BF)

    loads["feat"].wait()
    loads["wk"].wait()
    rows = mm(pick, own_keys(0, feat[0, 0, 0]))
    key_tab[0, pl.ds(0, A), :] = rows[:A]
    key_send[pl.ds(0, PLANE), :] = rows[A:]

    pl.semaphore_wait(barrier, len(around))
    plane(0, pos_send, 0, pos_tab, A, 1)
    plane(2, key_send, 0, key_tab.at[0], A, 1)

    loads["vs"].wait()
    lane_first = iota((1, FIRST), 1)
    label_row = lane_first
    for n in range(A // G, FIRST // G):
        label_row = label_row + jnp.where(lane_first >> 3 == n, LABELS[n] - n * G, 0)
    label_row = label_row.astype(F32)
    face_f = jnp.concatenate(
        [jnp.where(column(vs[0, 0, 0, f : f + 1, :]) == label_row, 1.0, 0.0) for f in range(2)],
        axis=0,
    )
    face = face_f.astype(BF)
    face_mine[...] = face_f
    for m, (dx, dy, _) in enumerate(MESSAGES):
        remote(4, face_mine, face_all.at[m], at(dx, dy, 0))

    mine = (iota((A, EDGES), 1) & (A - 1)) == iota((A, EDGES), 0)
    mine_f = jnp.where(mine, 1.0, 0.0)
    mine_b = mine_f.astype(BF)
    mine_s[...] = mine_f
    edge[pl.ds(ROWS, A), :] = mine_b
    edge[pl.ds(SELF, DEPTH - SELF), :] = jnp.zeros((DEPTH - SELF, EDGES), BF)
    dr_s[...] = jnp.zeros_like(dr_s)
    key_back[:, pl.ds(BACK, DEPTH - BACK), :] = jnp.zeros((LAYERS, DEPTH - BACK, C), F32)
    pos_back[pl.ds(BACK, DEPTH - BACK), :] = jnp.zeros((DEPTH - BACK, 128), F32)
    slot_pick = jnp.where((iota((S, EDGES), 1) >> 5) == iota((S, EDGES), 0), 1.0, 0.0).astype(BF)
    loads["nbr"].wait()
    nbr_all = mm(nbr[0, 0, 0].astype(F32).astype(BF), slot_pick)
    nbr_row = jnp.sum(jnp.where(mine, nbr_all, 0.0), axis=0, keepdims=True)
    loads["cnt"].wait()
    cnt_rows = jnp.broadcast_to(cnt[0, 0].astype(F32), (16, A)).astype(BF)
    cnt_row = mm(cnt_rows, mine_b)[0:1]
    live = jnp.where((iota((1, EDGES), 1) >> 5).astype(F32) < cnt_row, 1.0, 0.0)
    tile = iota((16, EDGES), 0)
    for n in range(ROWS // 16):
        low, high = LABELS[2 * n], LABELS[2 * n + 1]
        label = jnp.where(tile < G, tile + low, tile + (high - G)).astype(F32)
        edge[pl.ds(16 * n, 16), :] = jnp.where(nbr_row == label, 1.0, 0.0).astype(BF)

    arrived(0, pos_tab, A, PLANE)
    first = pos_tab[pl.ds(0, FIRST), :]
    rows = sum(mm(face, part) for part in split3(first))
    span = BOX_SIDE * nz
    low_shift = jnp.where(iz == 0, span, 0.0).astype(F32)
    high_shift = jnp.where(iz == nz - 1, -span, 0.0).astype(F32)
    shift = jnp.where(iota((2 * G, 128), 0) < G, low_shift, high_shift)
    pos_face[...] = rows + jnp.where(iota((2 * G, 128), 1) == 2, shift, 0.0)
    zone(1, pos_face, 0, pos_tab, FIRST)

    arrived(2, key_tab.at[0], A, PLANE)
    face_send[...] = mm(face, key_tab[0, pl.ds(0, FIRST), :].astype(BF))
    zone(3, face_send, 0, key_tab.at[0], FIRST)

    arrived(4, face_all, 0, len(MESSAGES))
    lane = iota((2 * G, FIRST), 1)
    parts, starts = [], [A]
    for _, _, quads in MESSAGES:
        starts.append(starts[-1] + G * len(quads))
    for m, (dx, dy) in enumerate(PLACES):
        if (dx, dy) == (0, 0):
            parts.append(jnp.where(lane < A, face_f, 0.0))
        else:
            to = PLACES.index((-dx, -dy))
            within = (lane >= starts[to]) & (lane < starts[to + 1])
            parts.append(jnp.where(within, face_all[m], 0.0))
    given = mm(jnp.concatenate(parts, axis=0).astype(BF), pick)
    pick_all[pl.ds(FIRST, ZONE), :] = given.astype(BF)
    pick_back[...] = jnp.concatenate(
        [pick_f[A:], given, jnp.zeros((DEPTH - BACK, A), F32)], axis=0
    ).T.astype(BF)

    loads["wq"].wait()
    query_s[0] = exact(mm, feat[0, 0, 0], wq[0])
    loads["wr"].wait()

    arrived(1, pos_tab, FIRST, 2 * G)
    place = jnp.concatenate(
        [pos_tab[...], -pos_tab[pl.ds(0, A), :], jnp.zeros((DEPTH - SELF, 128), F32)], axis=0
    )
    place_t = place.T[0:G, :]
    parts = [part.astype(F32) for part in split3(place_t)] + [jnp.zeros((G, DEPTH), F32)]
    offset = mm(jnp.concatenate(parts, axis=0).astype(BF), edge[...])
    offset = offset[0:G] + (offset[G : 2 * G] + offset[2 * G : 3 * G])
    dist = jnp.sqrt(jnp.sum(offset * offset, axis=0, keepdims=True) + SOFTEN)
    inv = 1.0 / dist
    scaled = dist * (1.0 / CUTOFF)
    gap = 1.0 - scaled * scaled
    inside = jnp.where(scaled < 1.0, live, 0.0)
    envelope = inside * gap * gap
    unit = offset * inv
    order = (iota((NB, EDGES), 0) + 1).astype(F32)
    turn = order * scaled
    whole = jnp.floor(turn + 0.5)
    angle = (turn - whole) * math.pi
    sign = 1.0 - 2.0 * (whole - 2.0 * jnp.floor(0.5 * whole))
    sq = angle * angle
    sine, cosine = jnp.zeros_like(sq), jnp.zeros_like(sq)
    for n in range(6, -1, -1):
        sine = sine * sq + (-1.0) ** n / math.factorial(2 * n + 1)
        cosine = cosine * sq + (-1.0) ** n / math.factorial(2 * n)
    inv_scaled = CUTOFF * inv
    basis = sign * sine * angle * inv_scaled
    dbasis_s[...] = (order * math.pi * sign * cosine - basis) * inv_scaled
    unit_s[...] = unit
    geo[...] = jnp.concatenate(
        [envelope, inv, -4.0 * inside * gap * scaled, jnp.zeros((5, EDGES), F32)], axis=0
    )
    basis_h, basis_l = split(basis)
    basis_h, basis_l = basis_h.astype(F32), basis_l.astype(F32)
    edge[pl.ds(SELF, 32), :] = jnp.concatenate(
        [basis_h, basis_l, basis_h, jnp.zeros_like(basis)], axis=0
    ).astype(BF)
    for q in range(4):
        row = envelope if q == 0 else envelope * unit[q - 1 : q]
        w_h, w_l = split(row * mine_s[...])
        weight[pl.ds(A * q, A), :] = w_h
        weight[pl.ds(4 * A + A * q, A), :] = w_l

    def forward(layer, h):
        radial_h, radial_l = split(wr[layer])
        radial_h, radial_l = radial_h.astype(F32), radial_l.astype(F32)
        rows = jnp.concatenate(
            [
                key_tab[layer],
                query_s[layer],
                radial_h,
                radial_h,
                radial_l,
                jnp.zeros((DEPTH - SELF - 3 * NB, C), F32),
            ],
            axis=0,
        )
        mt[...] = (0.5 * rows).T.astype(BF)
        for n in range(CHUNKS):
            part = pl.ds(n * STEP, STEP)
            half = mm(mt[...], edge[:, part])
            turned = jnp.tanh(half)
            more = 1.0 + turned
            act[layer, :, part] = (half * more).astype(BF)
            slope[layer, :, part] = more * (1.0 + half * (1.0 - turned))
        total = mm_nt(weight[...], act[layer])
        total = total[: 4 * A] + total[4 * A :]
        gather_h, gather_l = split(total[:A])
        vec_h, vec_l = split(total[A:])
        vec_s[layer] = FACTOR * (mm_nt(vec_h, wv[layer]) + mm_nt(vec_l, wv[layer]))
        return h + FACTOR * (mm(gather_h, wm[layer]) + mm(gather_l, wm[layer]))

    loads["wm"].wait()
    loads["wv"].wait()
    arrived(3, key_tab.at[0], FIRST, 2 * G)
    h1 = forward(0, feat[0, 0, 0])
    h1_s[...] = h1
    sent(2, key_send, 0, PLANE)
    rows = mm(pick_all[...], own_keys(1, h1))
    key_tab[1, pl.ds(0, A), :] = rows[:A]
    key_send[...] = rows[A:]
    zone_out(6, key_send, PLANE, zone_in)
    plane(5, key_send, 0, key_tab.at[1], A, 1)
    query_s[1] = exact(mm, h1_s[...], wq[1])
    loads["wh"].wait()
    loads["we"].wait()
    arrived(5, key_tab.at[1], A, PLANE)
    arrived(6, zone_in, 0, ZONE)
    zone_rows = zone_in[pl.ds(0, 2 * G), :]
    for m in range(1, len(PLACES)):
        zone_rows = zone_rows + zone_in[pl.ds(2 * G * m, 2 * G), :]
    key_tab[1, pl.ds(FIRST, 2 * G), :] = zone_rows
    h2 = forward(1, h1_s[...])
    h2_s[...] = h2

    lat = exact(mm, h2_s[...], wh[...])
    gate = 0.5 * jnp.tanh(0.5 * lat) + 0.5
    hidden = lat * gate
    readout = we[...]
    square = vec_s[0] * vec_s[0] + vec_s[1] * vec_s[1]
    square = square[:A] + (square[A : 2 * A] + square[2 * A :])
    energy = jnp.sum(hidden * readout, axis=1, keepdims=True) + jnp.sum(
        square, axis=1, keepdims=True
    ) * (1.0 / CT)
    en_out[0, 0] = jnp.sum(
        jnp.where(iota((A, A), 0) == iota((A, A), 1), energy, 0.0), axis=0, keepdims=True
    )
    dh_s[...] = exact(mm_nt, readout * (gate + hidden * (1.0 - gate)), wh[...])

    def backward(layer):
        dh_h, dh_l = split(dh_s[...])
        g0 = FACTOR * (mm_nt(dh_h, wm[layer]) + mm_nt(dh_l, wm[layer]))
        dv_h, dv_l = split(vec_s[layer] * (2.0 / CT))
        gx = FACTOR * (mm(dv_h, wv[layer]) + mm(dv_l, wv[layer]))
        pull = jnp.concatenate([g0, gx], axis=0)
        pull_b = pull.astype(BF)
        mp[...] = jnp.concatenate([0.5 * pull, 0.5 * pull], axis=0).T.astype(BF)
        radial_h, radial_l = split(wr[layer])
        radial = jnp.concatenate([radial_h.astype(F32), radial_l.astype(F32)], axis=0).astype(BF)
        for n in range(CHUNKS):
            part = pl.ds(n * STEP, STEP)
            dl = (mm(mp[...], weight[:, part]) * slope[layer, :, part]).astype(BF)
            dlat[:, part] = dl
            cross = mm(pull_b, act[layer, :, part])
            rows = [
                jnp.sum(cross[A * q : A * q + A] * mine_s[:, :STEP], axis=0, keepdims=True)
                for q in range(4)
            ]
            rows = jnp.concatenate(rows + [jnp.zeros((4, STEP), F32)], axis=0)
            got = mm(radial, dl)
            got = got[:NB] + got[NB:]
            if layer == LAYERS - 1:
                dw[:, part] = rows
                db[:, part] = got
            else:
                dw[:, part] += rows
                db[:, part] += got
        drows = mm_nt(edge[pl.ds(0, SELF), :], dlat[...])
        dkey[layer] = drows[:ROWS]
        give_back(7 + layer, dkey.at[layer], key_back.at[layer])
        dq_s[...] = dh_s[...] + exact(mm_nt, drows[ROWS:], wq[layer])

    def collect(own, back):
        back_h, back_l = split(back)
        return own + (mm(pick_back[...], back_h) + mm(pick_back[...], back_l))

    def finish(layer):
        arrived(7 + layer, key_back.at[layer], 0, BACK)
        own = collect(dkey[layer, pl.ds(0, A), :], key_back[layer])
        return dq_s[...] + exact(mm_nt, own, wk[layer])

    backward(1)
    dh_s[...] = finish(1)
    backward(0)

    envelope, inv, bend = geo[0:1], geo[1:2], geo[2:3]
    unit = unit_s[...]
    lanes = iota((G, EDGES), 0)
    du = jnp.zeros((G, EDGES), F32)
    for q in range(3):
        du = jnp.where(lanes == q, dw[q + 1 : q + 2], du)
    along = jnp.sum(du * unit, axis=0, keepdims=True)
    dscaled = bend * (dw[0:1] + along) + jnp.sum(db[...] * dbasis_s[...], axis=0, keepdims=True)
    ddist = dscaled * (1.0 / CUTOFF) - inv * envelope * along
    dr_h, dr_l = split(du * (envelope * inv) + unit * ddist)
    dr_s[pl.ds(0, 16), :] = jnp.concatenate([dr_h.astype(F32), dr_l.astype(F32)], axis=0).astype(BF)
    rows = mm_nt(edge[pl.ds(0, SELF), :], dr_s[...])
    pos_grad[...] = rows[:ROWS]
    give_back(9, pos_grad, pos_back)
    own_s[...] = rows[:A] - rows[ROWS:]

    grad_out[0, 0, 0] = finish(0)
    arrived(9, pos_back, 0, BACK)
    pos_own = collect(own_s[...], pos_back[...])
    pos_own = jnp.concatenate([pos_own, jnp.zeros((128 - A, 128), F32)], axis=0).T
    pos_own = -(pos_own[0:G, :A] + pos_own[G : 2 * G, :A])
    for q in range(3):
        force_out[q, 0, 0] = pos_own[q : q + 1]

    sent(0, pos_send, 0, PLANE)
    sent(1, pos_face, 0, 2 * G)
    sent(3, face_send, 0, 2 * G)
    sent(4, face_all, 0, len(MESSAGES))
    sent(5, key_send, 0, PLANE)
    sent(6, key_send, PLANE, ZONE)
    for layer in range(LAYERS):
        sent(7 + layer, key_back.at[layer], 0, BACK)
    sent(9, pos_back, 0, BACK)


def per_device(*args):
    hbm = pl.BlockSpec(memory_space=pltpu.HBM)
    vmem = pl.BlockSpec(memory_space=pltpu.VMEM)
    args = list(args)
    args[10] = args[10].swapaxes(1, 2)
    args[12] = args[12].reshape(1, C)
    f32, bf = (lambda *shape: pltpu.VMEM(shape, F32)), (lambda *shape: pltpu.VMEM(shape, BF))
    return pl.pallas_call(
        kernel,
        out_shape=(
            jax.ShapeDtypeStruct((1, 1, 1, A), F32),
            jax.ShapeDtypeStruct((3, 1, 1, 1, A), F32),
            jax.ShapeDtypeStruct((1, 1, 1, A, C), F32),
        ),
        in_specs=[hbm] * len(args),
        out_specs=(vmem,) * 3,
        scratch_shapes=[pltpu.VMEM(a.shape, a.dtype) for a in args]
        + [
            f32(2 * G, 128), f32(len(MESSAGES), 2 * G, 128), f32(ROWS, 128), f32(PLANE, 128),
            f32(2 * G, 128), f32(ROWS, 128), f32(DEPTH, 128),
            f32(LAYERS, ROWS, C), f32(BACK, C), f32(2 * G, C), f32(ZONE, C),
            f32(LAYERS, ROWS, C), f32(LAYERS, DEPTH, C),
            bf(FIRST + ZONE, A), bf(A, DEPTH), f32(A, EDGES), f32(8, EDGES), f32(G, EDGES),
            f32(NB, EDGES), bf(DEPTH, EDGES), bf(8 * A, EDGES), bf(LAYERS, C, EDGES),
            f32(LAYERS, C, EDGES), bf(C, EDGES),
            bf(C, C), bf(C, C), f32(8, EDGES), f32(NB, EDGES), bf(128, EDGES),
            f32(A, C), f32(A, C), f32(A, C), f32(A, C), f32(A, 128), f32(LAYERS, A, C),
            f32(LAYERS, 3 * A, CT),
            pltpu.SemaphoreType.DMA((13,)),
            pltpu.SemaphoreType.DMA((10,)),
            pltpu.SemaphoreType.DMA((10,)),
        ],
        compiler_params=pltpu.CompilerParams(
            collective_id=0, has_side_effects=True, vmem_limit_bytes=60 * 1024 * 1024
        ),
        cost_estimate=pl.CostEstimate(
            flops=2_500_000_000, bytes_accessed=2_000_000, transcendentals=800_000
        ),
    )(*args)


def solution(mesh):
    return jax.shard_map(
        per_device,
        mesh=mesh,
        in_specs=(
            P(None, "gx", "gy", "gz", None),
            P("gx", "gy", "gz", None, None),
            P("gx", "gy", "gz", None, None, None),
            P("gx", "gy", "gz", None, None),
            P("gx", "gy", "gz", None, None),
            P("gx", "gy", "gz", None),
            P(),
            P(),
            P(),
            P(),
            P(),
            P(),
            P(),
        ),
        out_specs=(
            P("gx", "gy", "gz", None),
            P(None, "gx", "gy", "gz", None),
            P("gx", "gy", "gz", None, None),
        ),
        check_vma=False,
    )
```

time: 64 us -> 48.2 us (0.75)
  Pallas kernels: 55.6 us -> 44.3 us
  local copies, waits for them, and re-layouts: 7.39 us -> 3.03 us
    pallas_call x1, Pallas kernels: 55.6 us -> 44.3 us  [per_device(): pl.pallas_call(kernel, out_shape=(jax.ShapeDtypeStruct((1, 1, 1, A), F32)...]
    unnamed x29 -> x7, local copies, waits for them, and re-layouts: 7.39 us -> 3.03 us
where the time goes in v1:
time: 48.2 us; the launch traced here: 48 us
  Pallas kernels  44.3 us (92%)
  local copies, waits for them, and re-layouts  3.03 us (6%)
  between operations  0.66 us (1%)
    pallas_call x1, Pallas kernels, per_device(): pl.pallas_call(kernel, out_shape=(jax.ShapeDtypeStruct((1, 1, 1, A), F32)...  44.3 us
    unnamed x7, local copies, waits for them, and re-layouts  3.03 us

profile of v1, /device:TPU:1, one launch (start us, length us, event | category | flops | bytes accessed | tf_op | source)
XLA Modules:
  0.0 48.0 jit_solution(17783466499373915116)
XLA Ops:
  0.6 44.3 %shard_map.148 = (f32[1,1,1,32]{3,2,1,0:T(1,128)}, f32[3,1,1,1,32]{4,3,2,1,0:T(1,128)}, f32[1,1,1,32,256]{4,3,2,1,0:T(8,128)}) custom-call(f32[3,1,1,1,32]{4,3,2,1,0:T(1,128)} %pos_in.1, f32[1,1,1,32,256]{4,3,2,1,0:T(8,128)} %feat_in.1, s32[1,1,1,2,2,8]{5,4,3,2,1,0:T(2,128)} %ps_in.1, s32[1,1,1,2,8]{4,3,2,1,0:T(2,128)} %vs_in.1, ...), custom_call_target="tpu_custom_call" | custom-call | flops 2500000000 | bytes 2000000 | tf_op jit(solution)/shard_map/pallas_call | solution.py:488
  44.9 0.0 copy-start.1
  44.9 0.0 copy-start
  44.9 0.6 %copy-done.1 = f32[1,1,1,32]{3,2,1,0:T(1,128)S(1)} copy-done((f32[1,1,1,32]{3,2,1,0:T(1,128)S(1)}, f32[1,1,1,32]{3,2,1,0:T(1,128)}, u32[]{:S(2)}) %copy-start.1) | copy-done | bytes 152
  45.5 0.5 %copy.19 = f32[1,1,1,32]{3,2,1,0:T(1,128)} copy(f32[1,1,1,32]{3,2,1,0:T(1,128)S(1)} %copy-done.1) | data formatting | bytes 256
  46.0 0.0 copy-done
  46.0 0.6 %copy.20 = f32[3,1,1,1,32]{4,3,2,1,0:T(1,128)} copy(f32[3,1,1,1,32]{4,3,2,1,0:T(1,128)S(1)} %copy-done) | data formatting | bytes 768
  46.6 1.4 %copy.21 = f32[1,1,1,32,256]{4,3,2,1,0:T(8,128)} copy(f32[1,1,1,32,256]{4,3,2,1,0:T(8,128)} %get-tuple-element.8) | data formatting | bytes 65536
Async XLA Ops:
  44.9 0.6 %copy-start.1 = (f32[1,1,1,32]{3,2,1,0:T(1,128)S(1)}, f32[1,1,1,32]{3,2,1,0:T(1,128)}, u32[]{:S(2)}) copy-start(f32[1,1,1,32]{3,2,1,0:T(1,128)} %get-tuple-element.6) | copy-start | bytes 388
  44.9 1.1 %copy-start = (f32[3,1,1,1,32]{4,3,2,1,0:T(1,128)S(1)}, f32[3,1,1,1,32]{4,3,2,1,0:T(1,128)}, u32[]{:S(2)}) copy-start(f32[3,1,1,1,32]{4,3,2,1,0:T(1,128)} %get-tuple-element.7) | copy-start | bytes 1156

commit v2 on v1

--- a/solution.py
+++ b/solution.py
@@ -73,10 +73,11 @@
     pos_in, feat_in, ps_in, vs_in, nbr_in, cnt_in, wq_in, wk_in, wr_in, wm_in, wv_in, wh_in, we_in,
     en_out, force_out, grad_out,
     pos, feat, ps, vs, nbr, cnt, wq, wk, wr, wm, wv, wh, we,
-    face_mine, face_all, pos_tab, pos_send, pos_face, pos_grad, pos_back,
-    key_tab, key_send, face_send, zone_in, dkey, key_back,
+    face_mine, face_all, pos_tab, pos_send, pos_face,
+    key_tab, key_send, face_send, zone_in, dkey_0, dkey_1, back_0, back_1,
     pick_all, pick_back, mine_s, geo, unit_s, dbasis_s, edge, weight, act, slope, dlat,
-    mt, mp, dw, db, dr_s, h1_s, h2_s, dh_s, dq_s, own_s, query_s, vec_s,
+    mt, mp, dw, db, base_s, base_t, dh_s, own_s, query_s, head_s, hidden_s,
+    pos_own_s, rest_s, gather_s, pull_s, joint, vec_s,
     load_sem, send_sem, recv_sem,
 ):
     ix, iy, iz = (lax.axis_index(n) for n in ("gx", "gy", "gz"))
@@ -235,9 +236,9 @@
     mine_s[...] = mine_f
     edge[pl.ds(ROWS, A), :] = mine_b
     edge[pl.ds(SELF, DEPTH - SELF), :] = jnp.zeros((DEPTH - SELF, EDGES), BF)
-    dr_s[...] = jnp.zeros_like(dr_s)
-    key_back[:, pl.ds(BACK, DEPTH - BACK), :] = jnp.zeros((LAYERS, DEPTH - BACK, C), F32)
-    pos_back[pl.ds(BACK, DEPTH - BACK), :] = jnp.zeros((DEPTH - BACK, 128), F32)
+    dlat[pl.ds(C, 128), :] = jnp.zeros((128, EDGES), BF)
+    for back in (back_0, back_1):
+        back[pl.ds(BACK, DEPTH - BACK), :] = jnp.zeros((DEPTH - BACK, back.shape[1]), F32)
     slot_pick = jnp.where((iota((S, EDGES), 1) >> 5) == iota((S, EDGES), 0), 1.0, 0.0).astype(BF)
     loads["nbr"].wait()
     nbr_all = mm(nbr[0, 0, 0].astype(F32).astype(BF), slot_pick)
@@ -246,12 +247,26 @@
     cnt_rows = jnp.broadcast_to(cnt[0, 0].astype(F32), (16, A)).astype(BF)
     cnt_row = mm(cnt_rows, mine_b)[0:1]
     live = jnp.where((iota((1, EDGES), 1) >> 5).astype(F32) < cnt_row, 1.0, 0.0)
-    tile = iota((16, EDGES), 0)
-    for n in range(ROWS // 16):
-        low, high = LABELS[2 * n], LABELS[2 * n + 1]
-        label = jnp.where(tile < G, tile + low, tile + (high - G)).astype(F32)
-        edge[pl.ds(16 * n, 16), :] = jnp.where(nbr_row == label, 1.0, 0.0).astype(BF)
-
+    def rest(layer, queries):
+        radial_h, radial_l = split(wr[layer])
+        radial_h, radial_l = radial_h.astype(F32), radial_l.astype(F32)
+        zeros = jnp.zeros((DEPTH - SELF - 3 * NB, C), F32)
+        rest_s[layer] = jnp.concatenate([queries, radial_h, radial_h, radial_l, zeros], axis=0)
+
+    loads["wq"].wait()
+    loads["wr"].wait()
+    loads["wm"].wait()
+    loads["wv"].wait()
+    loads["wh"].wait()
+    loads["we"].wait()
+    h0 = feat[0, 0, 0]
+    rest(0, exact(mm, h0, wq[0]))
+    base_s[...] = exact(mm, h0, wk[1])
+    for n, (mixing, after) in enumerate(((wm[0], wk[1]), (wm[1], wh[...]))):
+        after_h, after_l = split(after)
+        joint_h, joint_l = split(FACTOR * (mm(mixing, after_h) + mm(mixing, after_l)))
+        joint[2 * n] = joint_h
+        joint[2 * n + 1] = joint_l
     arrived(0, pos_tab, A, PLANE)
     first = pos_tab[pl.ds(0, FIRST), :]
     rows = sum(mm(face, part) for part in split3(first))
@@ -265,6 +280,12 @@
     arrived(2, key_tab.at[0], A, PLANE)
     face_send[...] = mm(face, key_tab[0, pl.ds(0, FIRST), :].astype(BF))
     zone(3, face_send, 0, key_tab.at[0], FIRST)
+
+    tile = iota((16, EDGES), 0)
+    for n in range(ROWS // 16):
+        low, high = LABELS[2 * n], LABELS[2 * n + 1]
+        label = jnp.where(tile < G, tile + low, tile + (high - G)).astype(F32)
+        edge[pl.ds(16 * n, 16), :] = jnp.where(nbr_row == label, 1.0, 0.0).astype(BF)
 
     arrived(4, face_all, 0, len(MESSAGES))
     lane = iota((2 * G, FIRST), 1)
@@ -283,10 +304,6 @@
     pick_back[...] = jnp.concatenate(
         [pick_f[A:], given, jnp.zeros((DEPTH - BACK, A), F32)], axis=0
     ).T.astype(BF)
-
-    loads["wq"].wait()
-    query_s[0] = exact(mm, feat[0, 0, 0], wq[0])
-    loads["wr"].wait()
 
     arrived(1, pos_tab, FIRST, 2 * G)
     place = jnp.concatenate(
@@ -331,137 +348,162 @@
         weight[pl.ds(A * q, A), :] = w_h
         weight[pl.ds(4 * A + A * q, A), :] = w_l
 
-    def forward(layer, h):
-        radial_h, radial_l = split(wr[layer])
-        radial_h, radial_l = radial_h.astype(F32), radial_l.astype(F32)
-        rows = jnp.concatenate(
-            [
-                key_tab[layer],
-                query_s[layer],
-                radial_h,
-                radial_h,
-                radial_l,
-                jnp.zeros((DEPTH - SELF - 3 * NB, C), F32),
-            ],
-            axis=0,
-        )
-        mt[...] = (0.5 * rows).T.astype(BF)
+    def near_keys(layer):
+        mt[:, pl.ds(0, FIRST)] = (0.5 * key_tab[layer, pl.ds(0, FIRST), :]).T.astype(BF)
+
+    def forward(layer, zone_rows):
+        rows = jnp.concatenate([zone_rows, rest_s[layer]], axis=0)
+        mt[:, pl.ds(FIRST, DEPTH - FIRST)] = (0.5 * rows).T.astype(BF)
         for n in range(CHUNKS):
             part = pl.ds(n * STEP, STEP)
             half = mm(mt[...], edge[:, part])
             turned = jnp.tanh(half)
             more = 1.0 + turned
-            act[layer, :, part] = (half * more).astype(BF)
+            active = (half * more).astype(BF)
+            act[layer, :, part] = active
             slope[layer, :, part] = more * (1.0 + half * (1.0 - turned))
         total = mm_nt(weight[...], act[layer])
         total = total[: 4 * A] + total[4 * A :]
-        gather_h, gather_l = split(total[:A])
-        vec_h, vec_l = split(total[A:])
-        vec_s[layer] = FACTOR * (mm_nt(vec_h, wv[layer]) + mm_nt(vec_l, wv[layer]))
-        return h + FACTOR * (mm(gather_h, wm[layer]) + mm(gather_l, wm[layer]))
-
-    loads["wm"].wait()
-    loads["wv"].wait()
+        gather_s[...] = total
+        return total
+
+    def vectors(layer):
+        vec_h, vec_l = split(gather_s[pl.ds(A, 3 * A), :])
+        vector = FACTOR * (mm_nt(vec_h, wv[layer]) + mm_nt(vec_l, wv[layer]))
+        vec_s[layer] = vector
+        dv_h, dv_l = split(vector * (2.0 / CT))
+        gx = FACTOR * (mm(dv_h, wv[layer]) + mm(dv_l, wv[layer]))
+        pull_s[layer, pl.ds(A, 3 * A), :] = gx.astype(BF)
+        flipped = jnp.concatenate([jnp.zeros((A, C), F32), 0.5 * gx], axis=0).T.astype(BF)
+        mp[layer, :, pl.ds(0, 4 * A)] = flipped
+        mp[layer, :, pl.ds(4 * A, 4 * A)] = flipped
+
+    def thrice(product, a, b_h, b_l):
+        a_h, a_l = split(a)
+        return product(a_h, b_h) + (product(a_h, b_l) + product(a_l, b_h))
+
+    near_keys(0)
+
     arrived(3, key_tab.at[0], FIRST, 2 * G)
-    h1 = forward(0, feat[0, 0, 0])
-    h1_s[...] = h1
+    total = forward(0, key_tab[0, pl.ds(FIRST, 2 * G), :])
+    keys = base_s[...] + thrice(mm, total[:A], joint[0], joint[1])
+    rows = mm(pick_all[...], keys.astype(BF))
+    key_tab[1, pl.ds(0, A), :] = rows[:A]
     sent(2, key_send, 0, PLANE)
-    rows = mm(pick_all[...], own_keys(1, h1))
-    key_tab[1, pl.ds(0, A), :] = rows[:A]
     key_send[...] = rows[A:]
     zone_out(6, key_send, PLANE, zone_in)
     plane(5, key_send, 0, key_tab.at[1], A, 1)
-    query_s[1] = exact(mm, h1_s[...], wq[1])
-    loads["wh"].wait()
-    loads["we"].wait()
+
+    gather_h, gather_l = split(gather_s[pl.ds(0, A), :])
+    h1 = feat[0, 0, 0] + FACTOR * (mm(gather_h, wm[0]) + mm(gather_l, wm[0]))
+    rest(1, exact(mm, h1, wq[1]))
+    base_s[...] = exact(mm, h1, wh[...])
+    vectors(0)
     arrived(5, key_tab.at[1], A, PLANE)
+    near_keys(1)
     arrived(6, zone_in, 0, ZONE)
     zone_rows = zone_in[pl.ds(0, 2 * G), :]
     for m in range(1, len(PLACES)):
         zone_rows = zone_rows + zone_in[pl.ds(2 * G * m, 2 * G), :]
-    key_tab[1, pl.ds(FIRST, 2 * G), :] = zone_rows
-    h2 = forward(1, h1_s[...])
-    h2_s[...] = h2
-
-    lat = exact(mm, h2_s[...], wh[...])
+    total = forward(1, zone_rows)
+
+    lat = base_s[...] + thrice(mm, total[:A], joint[2], joint[3])
     gate = 0.5 * jnp.tanh(0.5 * lat) + 0.5
     hidden = lat * gate
     readout = we[...]
-    square = vec_s[0] * vec_s[0] + vec_s[1] * vec_s[1]
-    square = square[:A] + (square[A : 2 * A] + square[2 * A :])
-    energy = jnp.sum(hidden * readout, axis=1, keepdims=True) + jnp.sum(
-        square, axis=1, keepdims=True
-    ) * (1.0 / CT)
-    en_out[0, 0] = jnp.sum(
-        jnp.where(iota((A, A), 0) == iota((A, A), 1), energy, 0.0), axis=0, keepdims=True
-    )
-    dh_s[...] = exact(mm_nt, readout * (gate + hidden * (1.0 - gate)), wh[...])
+    dhead = readout * (gate + hidden * (1.0 - gate))
+    head_s[...] = dhead
+    hidden_s[...] = hidden * readout
+    vectors(1)
+
+    def set_pull(layer, g0, g0_t):
+        pull_s[layer, pl.ds(0, A), :] = g0.astype(BF)
+        half = (0.5 * g0_t).astype(BF)
+        mp[layer, :, pl.ds(0, A)] = half
+        mp[layer, :, pl.ds(4 * A, A)] = half
+
+    def flip(a, b):
+        return mm_nt(b, a)
+
+    def places(part, du, dbasis):
+        unit, inv = unit_s[:, part], geo[1:2, part]
+        along = jnp.sum(du * unit, axis=0, keepdims=True)
+        dscaled = geo[2:3, part] * (du[3:4] + along) + jnp.sum(
+            dbasis * dbasis_s[:, part], axis=0, keepdims=True
+        )
+        spread = geo[0:1, part] * inv
+        return du * spread + unit * (dscaled * (1.0 / CUTOFF) - spread * along)
 
     def backward(layer):
-        dh_h, dh_l = split(dh_s[...])
-        g0 = FACTOR * (mm_nt(dh_h, wm[layer]) + mm_nt(dh_l, wm[layer]))
-        dv_h, dv_l = split(vec_s[layer] * (2.0 / CT))
-        gx = FACTOR * (mm(dv_h, wv[layer]) + mm(dv_l, wv[layer]))
-        pull = jnp.concatenate([g0, gx], axis=0)
-        pull_b = pull.astype(BF)
-        mp[...] = jnp.concatenate([0.5 * pull, 0.5 * pull], axis=0).T.astype(BF)
         radial_h, radial_l = split(wr[layer])
         radial = jnp.concatenate([radial_h.astype(F32), radial_l.astype(F32)], axis=0).astype(BF)
         for n in range(CHUNKS):
             part = pl.ds(n * STEP, STEP)
-            dl = (mm(mp[...], weight[:, part]) * slope[layer, :, part]).astype(BF)
-            dlat[:, part] = dl
-            cross = mm(pull_b, act[layer, :, part])
+            dl = (mm(mp[layer], weight[:, part]) * slope[layer, :, part]).astype(BF)
+            dlat[pl.ds(0, C), part] = dl
+            cross = mm(pull_s[layer], act[layer, :, part])
             rows = [
                 jnp.sum(cross[A * q : A * q + A] * mine_s[:, :STEP], axis=0, keepdims=True)
                 for q in range(4)
             ]
-            rows = jnp.concatenate(rows + [jnp.zeros((4, STEP), F32)], axis=0)
+            rows = jnp.concatenate(rows[1:] + rows[:1] + [jnp.zeros((4, STEP), F32)], axis=0)
             got = mm(radial, dl)
             got = got[:NB] + got[NB:]
             if layer == LAYERS - 1:
                 dw[:, part] = rows
                 db[:, part] = got
             else:
-                dw[:, part] += rows
-                db[:, part] += got
-        drows = mm_nt(edge[pl.ds(0, SELF), :], dlat[...])
-        dkey[layer] = drows[:ROWS]
-        give_back(7 + layer, dkey.at[layer], key_back.at[layer])
-        dq_s[...] = dh_s[...] + exact(mm_nt, drows[ROWS:], wq[layer])
+                dr_h, dr_l = split(places(part, dw[:, part] + rows, db[:, part] + got))
+                both = jnp.concatenate([dr_h.astype(F32), dr_l.astype(F32)], axis=0)
+                dlat[pl.ds(C, 2 * G), part] = both.astype(BF)
+        mine, back = (dkey_0, back_0) if layer == 0 else (dkey_1, back_1)
+        drows = mm_nt(edge[pl.ds(0, SELF), :], dlat[pl.ds(0, mine.shape[1]), :])
+        mine[...] = drows[:ROWS]
+        give_back(7 + layer, mine, back)
+        query_s[...] = drows[ROWS:, :C]
+        if layer == 0:
+            pos_own_s[...] = drows[ROWS:, C:]
 
     def collect(own, back):
         back_h, back_l = split(back)
         return own + (mm(pick_back[...], back_h) + mm(pick_back[...], back_l))
 
-    def finish(layer):
-        arrived(7 + layer, key_back.at[layer], 0, BACK)
-        own = collect(dkey[layer, pl.ds(0, A), :], key_back[layer])
-        return dq_s[...] + exact(mm_nt, own, wk[layer])
-
+    def returned(layer):
+        mine, back = (dkey_0, back_0) if layer == 0 else (dkey_1, back_1)
+        arrived(7 + layer, back, 0, BACK)
+        return collect(mine[pl.ds(0, A), :], back[...])
+
+    set_pull(1, thrice(mm_nt, dhead, joint[2], joint[3]), thrice(flip, dhead, joint[2], joint[3]))
     backward(1)
-    dh_s[...] = finish(1)
+
+    square = vec_s[0] * vec_s[0] + vec_s[1] * vec_s[1]
+    square = square[:A] + (square[A : 2 * A] + square[2 * A :])
+    energy = jnp.sum(hidden_s[...], axis=1, keepdims=True) + jnp.sum(
+        square, axis=1, keepdims=True
+    ) * (1.0 / CT)
+    en_out[0, 0] = jnp.sum(
+        jnp.where(iota((A, A), 0) == iota((A, A), 1), energy, 0.0), axis=0, keepdims=True
+    )
+    dh = exact(mm_nt, head_s[...], wh[...]) + exact(mm_nt, query_s[...], wq[1])
+    dh_s[...] = dh
+    dh_h, dh_l = split(FACTOR * dh)
+    base_s[...] = mm_nt(dh_h, wm[0]) + mm_nt(dh_l, wm[0])
+    base_t[...] = mm_nt(wm[0], dh_h) + mm_nt(wm[0], dh_l)
+
+    own = returned(1)
+    set_pull(
+        0,
+        base_s[...] + thrice(mm_nt, own, joint[0], joint[1]),
+        base_t[...] + thrice(flip, own, joint[0], joint[1]),
+    )
+    own_s[...] = own
     backward(0)
 
-    envelope, inv, bend = geo[0:1], geo[1:2], geo[2:3]
-    unit = unit_s[...]
-    lanes = iota((G, EDGES), 0)
-    du = jnp.zeros((G, EDGES), F32)
-    for q in range(3):
-        du = jnp.where(lanes == q, dw[q + 1 : q + 2], du)
-    along = jnp.sum(du * unit, axis=0, keepdims=True)
-    dscaled = bend * (dw[0:1] + along) + jnp.sum(db[...] * dbasis_s[...], axis=0, keepdims=True)
-    ddist = dscaled * (1.0 / CUTOFF) - inv * envelope * along
-    dr_h, dr_l = split(du * (envelope * inv) + unit * ddist)
-    dr_s[pl.ds(0, 16), :] = jnp.concatenate([dr_h.astype(F32), dr_l.astype(F32)], axis=0).astype(BF)
-    rows = mm_nt(edge[pl.ds(0, SELF), :], dr_s[...])
-    pos_grad[...] = rows[:ROWS]
-    give_back(9, pos_grad, pos_back)
-    own_s[...] = rows[:A] - rows[ROWS:]
-
-    grad_out[0, 0, 0] = finish(0)
-    arrived(9, pos_back, 0, BACK)
-    pos_own = collect(own_s[...], pos_back[...])
+    dh = dh_s[...] + exact(mm_nt, own_s[...], wk[1])
+    dh_s[...] = dh + exact(mm_nt, query_s[...], wq[0])
+    own = returned(0)
+    grad_out[0, 0, 0] = dh_s[...] + exact(mm_nt, own[:, :C], wk[0])
+    pos_own = own[:, C:] - pos_own_s[...]
     pos_own = jnp.concatenate([pos_own, jnp.zeros((128 - A, 128), F32)], axis=0).T
     pos_own = -(pos_own[0:G, :A] + pos_own[G : 2 * G, :A])
     for q in range(3):
@@ -473,9 +515,14 @@
     sent(4, face_all, 0, len(MESSAGES))
     sent(5, key_send, 0, PLANE)
     sent(6, key_send, PLANE, ZONE)
-    for layer in range(LAYERS):
-        sent(7 + layer, key_back.at[layer], 0, BACK)
-    sent(9, pos_back, 0, BACK)
+    sent(7, back_0, 0, BACK)
+    sent(8, back_1, 0, BACK)
+
+
+def hand_on(en_in, force_in, grad_in, en_out, force_out, grad_out, sem):
+    grad_out[...] = grad_in[...]
+    force_out[...] = force_in[...]
+    en_out[...] = en_in[...]
 
 
 def per_device(*args):
@@ -485,30 +532,32 @@
     args[10] = args[10].swapaxes(1, 2)
     args[12] = args[12].reshape(1, C)
     f32, bf = (lambda *shape: pltpu.VMEM(shape, F32)), (lambda *shape: pltpu.VMEM(shape, BF))
-    return pl.pallas_call(
+    out_shape = (
+        jax.ShapeDtypeStruct((1, 1, 1, A), F32),
+        jax.ShapeDtypeStruct((3, 1, 1, 1, A), F32),
+        jax.ShapeDtypeStruct((1, 1, 1, A, C), F32),
+    )
+    results = pl.pallas_call(
         kernel,
-        out_shape=(
-            jax.ShapeDtypeStruct((1, 1, 1, A), F32),
-            jax.ShapeDtypeStruct((3, 1, 1, 1, A), F32),
-            jax.ShapeDtypeStruct((1, 1, 1, A, C), F32),
-        ),
+        out_shape=out_shape,
         in_specs=[hbm] * len(args),
         out_specs=(vmem,) * 3,
         scratch_shapes=[pltpu.VMEM(a.shape, a.dtype) for a in args]
         + [
             f32(2 * G, 128), f32(len(MESSAGES), 2 * G, 128), f32(ROWS, 128), f32(PLANE, 128),
-            f32(2 * G, 128), f32(ROWS, 128), f32(DEPTH, 128),
+            f32(2 * G, 128),
             f32(LAYERS, ROWS, C), f32(BACK, C), f32(2 * G, C), f32(ZONE, C),
-            f32(LAYERS, ROWS, C), f32(LAYERS, DEPTH, C),
+            f32(ROWS, C + 128), f32(ROWS, C), f32(DEPTH, C + 128), f32(DEPTH, C),
             bf(FIRST + ZONE, A), bf(A, DEPTH), f32(A, EDGES), f32(8, EDGES), f32(G, EDGES),
             f32(NB, EDGES), bf(DEPTH, EDGES), bf(8 * A, EDGES), bf(LAYERS, C, EDGES),
-            f32(LAYERS, C, EDGES), bf(C, EDGES),
-            bf(C, C), bf(C, C), f32(8, EDGES), f32(NB, EDGES), bf(128, EDGES),
-            f32(A, C), f32(A, C), f32(A, C), f32(A, C), f32(A, 128), f32(LAYERS, A, C),
-            f32(LAYERS, 3 * A, CT),
+            f32(LAYERS, C, EDGES), bf(C + 128, EDGES),
+            bf(C, DEPTH), bf(LAYERS, C, 8 * A), f32(8, EDGES), f32(NB, EDGES),
+            f32(A, C), f32(C, A), f32(A, C), f32(A, C), f32(A, C), f32(A, C), f32(A, C),
+            f32(A, 128), f32(LAYERS, DEPTH - ROWS, C), f32(4 * A, C), bf(LAYERS, 4 * A, C),
+            bf(4, C, C), f32(LAYERS, 3 * A, CT),
             pltpu.SemaphoreType.DMA((13,)),
-            pltpu.SemaphoreType.DMA((10,)),
-            pltpu.SemaphoreType.DMA((10,)),
+            pltpu.SemaphoreType.DMA((9,)),
+            pltpu.SemaphoreType.DMA((9,)),
         ],
         compiler_params=pltpu.CompilerParams(
             collective_id=0, has_side_effects=True, vmem_limit_bytes=60 * 1024 * 1024
@@ -517,6 +566,14 @@
             flops=2_500_000_000, bytes_accessed=2_000_000, transcendentals=800_000
         ),
     )(*args)
+    return pl.pallas_call(
+        hand_on,
+        out_shape=out_shape,
+        in_specs=[vmem] * 3,
+        out_specs=(vmem,) * 3,
+        scratch_shapes=[pltpu.SemaphoreType.DMA((3,))],
+        compiler_params=pltpu.CompilerParams(vmem_limit_bytes=60 * 1024 * 1024),
+    )(*results)
 
 
 def solution(mesh):

time: 48.2 us -> 45.6 us (0.946)
  local copies, waits for them, and re-layouts: 3.03 us -> 0 us
    unnamed x7 -> x0, local copies, waits for them, and re-layouts: 3.03 us -> none
    pallas_call x1 -> x2, Pallas kernels: 44.3 us -> 44.7 us  [the longest x1 43.3 us: per_device(): pl.pallas_call(kernel, out_shape=out_shape, in_specs=[hbm] * len(args), o...]
where the time goes in v2:
time: 45.6 us; the launch traced here: 45.4 us
  Pallas kernels  44.7 us (98%)
  between operations  0.64 us (1%)
    pallas_call x1, Pallas kernels, per_device(): pl.pallas_call(kernel, out_shape=out_shape, in_specs=[hbm] * len(args), o...  43.3 us
    pallas_call x1, Pallas kernels, per_device(): pl.pallas_call(hand_on, out_shape=out_shape, in_specs=[vmem] * 3, out_spe...  1.42 us

profile of v2, /device:TPU:1, one launch (start us, length us, event | category | flops | bytes accessed | tf_op | source)
XLA Modules:
  0.0 45.4 jit_solution(18081063854742739360)
XLA Ops:
  0.6 43.3 %shard_map.148 = (f32[1,1,1,32]{3,2,1,0:T(1,128)}, f32[3,1,1,1,32]{4,3,2,1,0:T(1,128)}, f32[1,1,1,32,256]{4,3,2,1,0:T(8,128)}) custom-call(f32[3,1,1,1,32]{4,3,2,1,0:T(1,128)} %pos_in.1, f32[1,1,1,32,256]{4,3,2,1,0:T(8,128)} %feat_in.1, s32[1,1,1,2,2,8]{5,4,3,2,1,0:T(2,128)} %ps_in.1, s32[1,1,1,2,8]{4,3,2,1,0:T(2,128)} %vs_in.1, ...), custom_call_target="tpu_custom_call" | custom-call | flops 2500000000 | bytes 2000000 | tf_op jit(solution)/shard_map/pallas_call | solution.py:540
  44.0 1.4 %shard_map.149 = (f32[1,1,1,32]{3,2,1,0:T(1,128)}, f32[3,1,1,1,32]{4,3,2,1,0:T(1,128)}, f32[1,1,1,32,256]{4,3,2,1,0:T(8,128)}) custom-call(f32[1,1,1,32]{3,2,1,0:T(1,128)} %get-tuple-element.6.en_in, f32[3,1,1,1,32]{4,3,2,1,0:T(1,128)} %get-tuple-element.7.force_in, f32[1,1,1,32,256]{4,3,2,1,0:T(8,128)} %get-tuple-element.8.grad_in), custom_call_target="tpu_custom_call" | custom-call | tf_op jit(solution)/shard_map/pallas_call | solution.py:569

commit v3 on v2

--- a/solution.py
+++ b/solution.py
@@ -18,14 +18,15 @@
 
 MESSAGES = (
     (1, 0, ((1, 0), (1, 1))),
+    (1, 1, ((1, 1),)),
+    (1, -1, ((1, 0),)),
     (-1, 0, ((0, 0), (0, 1))),
+    (-1, 1, ((0, 1),)),
+    (-1, -1, ((0, 0),)),
     (0, 1, ((0, 1), (1, 1))),
     (0, -1, ((0, 0), (1, 0))),
-    (1, 1, ((1, 1),)),
-    (1, -1, ((1, 0),)),
-    (-1, 1, ((0, 1),)),
-    (-1, -1, ((0, 0),)),
 )
+SIDES = (1, -1, 0)
 BLOCKS = tuple((dx, dy, a, b) for dx, dy, quads in MESSAGES for a, b in quads)
 PLANE = G * len(BLOCKS)
 FIRST = A + PLANE
@@ -38,6 +39,7 @@
 PLACES = tuple((dx, dy) for dx, dy, _ in MESSAGES) + ((0, 0),)
 ZONE = 2 * G * len(PLACES)
 BACK = PLANE + ZONE
+PLANE_PART, ZONE_PART = PLANE // 3, ZONE // 3
 
 
 def mm(a, b):
@@ -89,6 +91,31 @@
             "gy": lax.rem(iy + (dy + ny), ny),
             "gz": lax.rem(iz + (dz + nz), nz),
         }
+
+    def beside(side, action):
+        if side == 0:
+            pl.when(ix >= 0)(action)
+        elif side == 1:
+            pl.when(ix < nx - 1)(action)
+        else:
+            pl.when(ix > 0)(action)
+
+    barrier = pltpu.get_barrier_semaphore()
+
+    def greet(where):
+        pl.semaphore_signal(barrier, inc=1, device_id=where, device_id_type=pl.DeviceIdType.MESH)
+
+    greet(at(0, 0, -1))
+    greet(at(0, 0, 1))
+    for side in SIDES:
+
+        def greet_side(side=side):
+            for dx, dy, _ in MESSAGES:
+                if dx == side:
+                    greet(at(dx, dy, 0))
+
+        beside(side, greet_side)
+    greeted = 4 + 3 * (ix > 0).astype(jnp.int32) + 3 * (ix < nx - 1).astype(jnp.int32)
 
     loads = {}
     for n, (name, src, dst) in enumerate(
@@ -111,68 +138,118 @@
         loads[name] = pltpu.make_async_copy(src, dst, load_sem.at[n])
         loads[name].start()
 
-    barrier = pltpu.get_barrier_semaphore()
-    around = [(dx, dy, 0) for dx, dy, _ in MESSAGES] + [(0, 0, -1), (0, 0, 1)]
-    for step in around:
-        pl.semaphore_signal(barrier, inc=1, device_id=at(*step), device_id_type=pl.DeviceIdType.MESH)
-
-    def remote(stage, src, dst, where):
+    def remote(stage, group, src, dst, where):
         pltpu.make_async_remote_copy(
             src_ref=src,
             dst_ref=dst,
-            send_sem=send_sem.at[stage],
-            recv_sem=recv_sem.at[stage],
+            send_sem=send_sem.at[stage, group],
+            recv_sem=recv_sem.at[stage, group],
             device_id=where,
             device_id_type=pl.DeviceIdType.MESH,
         ).start()
 
     def plane(stage, src, src_at, dst, dst_at, sign):
-        row = 0
-        for dx, dy, quads in MESSAGES:
-            rows = G * len(quads)
-            remote(
-                stage,
-                src.at[pl.ds(src_at + row, rows)],
-                dst.at[pl.ds(dst_at + row, rows)],
-                at(sign * dx, sign * dy, 0),
-            )
-            row += rows
+        for group, side in enumerate(SIDES):
+
+            def send(group=group, side=side):
+                row = 0
+                for dx, dy, quads in MESSAGES:
+                    rows = G * len(quads)
+                    if dx == side:
+                        remote(
+                            stage,
+                            group,
+                            src.at[pl.ds(src_at + row, rows)],
+                            dst.at[pl.ds(dst_at + row, rows)],
+                            at(sign * dx, sign * dy, 0),
+                        )
+                    row += rows
+
+            beside(sign * side, send)
 
     def zone(stage, src, src_at, dst, dst_at):
-        remote(stage, src.at[pl.ds(src_at, G)], dst.at[pl.ds(dst_at + G, G)], at(0, 0, -1))
-        remote(stage, src.at[pl.ds(src_at + G, G)], dst.at[pl.ds(dst_at, G)], at(0, 0, 1))
+        remote(stage, 0, src.at[pl.ds(src_at, G)], dst.at[pl.ds(dst_at + G, G)], at(0, 0, -1))
+        remote(stage, 0, src.at[pl.ds(src_at + G, G)], dst.at[pl.ds(dst_at, G)], at(0, 0, 1))
 
     def zone_out(stage, src, src_at, dst):
-        for m, (dx, dy) in enumerate(PLACES):
-            for f, dz in ((0, -1), (1, 1)):
-                remote(
-                    stage,
-                    src.at[pl.ds(src_at + (2 * m + f) * G, G)],
-                    dst.at[pl.ds((2 * m + 1 - f) * G, G)],
-                    at(-dx, -dy, dz),
-                )
+        for group, side in enumerate(SIDES):
+
+            def send(group=group, side=side):
+                for m, (dx, dy) in enumerate(PLACES):
+                    for f, dz in ((0, -1), (1, 1)):
+                        if dx == side:
+                            remote(
+                                stage,
+                                group,
+                                src.at[pl.ds(src_at + (2 * m + f) * G, G)],
+                                dst.at[pl.ds((2 * m + 1 - f) * G, G)],
+                                at(-dx, -dy, dz),
+                            )
+
+            beside(-side, send)
 
     def give_back(stage, src, dst):
-        for m, (dx, dy) in enumerate(PLACES):
-            for b, dz in ((0, -1), (1, 1)):
-                remote(
-                    stage,
-                    src.at[pl.ds(FIRST + b * G, G)],
-                    dst.at[pl.ds(PLANE + (2 * m + 1 - b) * G, G)],
-                    at(dx, dy, dz),
-                )
-        plane(stage, src, A, dst, 0, -1)
-
-    def arrived(stage, buf, row, rows):
-        part = buf.at[pl.ds(row, rows)]
+        for group, side in enumerate(SIDES):
+
+            def send(group=group, side=side):
+                for m, (dx, dy) in enumerate(PLACES):
+                    for b, dz in ((0, -1), (1, 1)):
+                        if dx == side:
+                            remote(
+                                stage,
+                                group,
+                                src.at[pl.ds(FIRST + b * G, G)],
+                                dst.at[pl.ds(PLANE + (2 * m + 1 - b) * G, G)],
+                                at(dx, dy, dz),
+                            )
+
+            beside(side, send)
+        plane(stage + 1, src, A, dst, 0, -1)
+
+    def arrived(stage, buf, row, rows, sign):
+        for group, side in enumerate(SIDES):
+            part = buf.at[pl.ds(row + rows * group, rows)]
+
+            def wait(group=group, part=part):
+                pltpu.make_async_copy(part, part, recv_sem.at[stage, group]).wait()
+
+            beside(sign * side, wait)
+
+    def sent(stage, buf, row, rows, sign):
+        for group, side in enumerate(SIDES):
+            part = buf.at[pl.ds(row + rows * group, rows)]
+
+            def wait(group=group, part=part):
+                pltpu.make_async_copy(part, part, send_sem.at[stage, group]).wait()
+
+            beside(sign * side, wait)
+
+    def arrived_zone(stage, buf):
+        part = buf.at[pl.ds(FIRST, 2 * G)]
 
         @pl.when(ix >= 0)
         def _():
-            pltpu.make_async_copy(part, part, recv_sem.at[stage]).wait()
-
-    def sent(stage, buf, row, rows):
-        part = buf.at[pl.ds(row, rows)]
-        pltpu.make_async_copy(part, part, send_sem.at[stage]).wait()
+            pltpu.make_async_copy(part, part, recv_sem.at[stage, 0]).wait()
+
+    def sent_zone(stage, buf):
+        part = buf.at[pl.ds(0, 2 * G)]
+        pltpu.make_async_copy(part, part, send_sem.at[stage, 0]).wait()
+
+    def clear(group):
+        def fill(buf, row, rows):
+            buf[pl.ds(row, rows)] = jnp.zeros((rows,) + buf.shape[1:], F32)
+
+        fill(pos_tab, A + PLANE_PART * group, PLANE_PART)
+        fill(face_all, 3 * group, 3)
+        fill(zone_in, ZONE_PART * (1 - group), ZONE_PART)
+        for layer in range(LAYERS):
+            fill(key_tab.at[layer], A + PLANE_PART * group, PLANE_PART)
+        for back in (back_0, back_1):
+            fill(back, PLANE + ZONE_PART * group, ZONE_PART)
+            fill(back, PLANE_PART * (1 - group), PLANE_PART)
+
+    pl.when(ix == 0)(lambda: clear(0))
+    pl.when(ix == nx - 1)(lambda: clear(1))
 
     sub8, lane8 = iota((G, G), 0), iota((G, G), 1)
 
@@ -211,7 +288,7 @@
     key_tab[0, pl.ds(0, A), :] = rows[:A]
     key_send[pl.ds(0, PLANE), :] = rows[A:]
 
-    pl.semaphore_wait(barrier, len(around))
+    pl.semaphore_wait(barrier, greeted)
     plane(0, pos_send, 0, pos_tab, A, 1)
     plane(2, key_send, 0, key_tab.at[0], A, 1)
 
@@ -227,8 +304,14 @@
     )
     face = face_f.astype(BF)
     face_mine[...] = face_f
-    for m, (dx, dy, _) in enumerate(MESSAGES):
-        remote(4, face_mine, face_all.at[m], at(dx, dy, 0))
+    for group, side in enumerate(SIDES):
+
+        def send_face(group=group, side=side):
+            for m, (dx, dy, _) in enumerate(MESSAGES):
+                if dx == side:
+                    remote(4, group, face_mine, face_all.at[m], at(dx, dy, 0))
+
+        beside(side, send_face)
 
     mine = (iota((A, EDGES), 1) & (A - 1)) == iota((A, EDGES), 0)
     mine_f = jnp.where(mine, 1.0, 0.0)
@@ -267,7 +350,7 @@
         joint_h, joint_l = split(FACTOR * (mm(mixing, after_h) + mm(mixing, after_l)))
         joint[2 * n] = joint_h
         joint[2 * n + 1] = joint_l
-    arrived(0, pos_tab, A, PLANE)
+    arrived(0, pos_tab, A, PLANE_PART, -1)
     first = pos_tab[pl.ds(0, FIRST), :]
     rows = sum(mm(face, part) for part in split3(first))
     span = BOX_SIDE * nz
@@ -277,7 +360,7 @@
     pos_face[...] = rows + jnp.where(iota((2 * G, 128), 1) == 2, shift, 0.0)
     zone(1, pos_face, 0, pos_tab, FIRST)
 
-    arrived(2, key_tab.at[0], A, PLANE)
+    arrived(2, key_tab.at[0], A, PLANE_PART, -1)
     face_send[...] = mm(face, key_tab[0, pl.ds(0, FIRST), :].astype(BF))
     zone(3, face_send, 0, key_tab.at[0], FIRST)
 
@@ -287,7 +370,13 @@
         label = jnp.where(tile < G, tile + low, tile + (high - G)).astype(F32)
         edge[pl.ds(16 * n, 16), :] = jnp.where(nbr_row == label, 1.0, 0.0).astype(BF)
 
-    arrived(4, face_all, 0, len(MESSAGES))
+    for group, side in enumerate(SIDES):
+        slots = face_all.at[pl.ds(3 * group, 2 if side == 0 else 3)]
+
+        def wait_face(group=group, slots=slots):
+            pltpu.make_async_copy(slots, slots, recv_sem.at[4, group]).wait()
+
+        beside(-side, wait_face)
     lane = iota((2 * G, FIRST), 1)
     parts, starts = [], [A]
     for _, _, quads in MESSAGES:
@@ -305,7 +394,7 @@
         [pick_f[A:], given, jnp.zeros((DEPTH - BACK, A), F32)], axis=0
     ).T.astype(BF)
 
-    arrived(1, pos_tab, FIRST, 2 * G)
+    arrived_zone(1, pos_tab)
     place = jnp.concatenate(
         [pos_tab[...], -pos_tab[pl.ds(0, A), :], jnp.zeros((DEPTH - SELF, 128), F32)], axis=0
     )
@@ -384,12 +473,12 @@
 
     near_keys(0)
 
-    arrived(3, key_tab.at[0], FIRST, 2 * G)
+    arrived_zone(3, key_tab.at[0])
     total = forward(0, key_tab[0, pl.ds(FIRST, 2 * G), :])
     keys = base_s[...] + thrice(mm, total[:A], joint[0], joint[1])
     rows = mm(pick_all[...], keys.astype(BF))
     key_tab[1, pl.ds(0, A), :] = rows[:A]
-    sent(2, key_send, 0, PLANE)
+    sent(2, key_send, 0, PLANE_PART, 1)
     key_send[...] = rows[A:]
     zone_out(6, key_send, PLANE, zone_in)
     plane(5, key_send, 0, key_tab.at[1], A, 1)
@@ -399,9 +488,9 @@
     rest(1, exact(mm, h1, wq[1]))
     base_s[...] = exact(mm, h1, wh[...])
     vectors(0)
-    arrived(5, key_tab.at[1], A, PLANE)
+    arrived(5, key_tab.at[1], A, PLANE_PART, -1)
     near_keys(1)
-    arrived(6, zone_in, 0, ZONE)
+    arrived(6, zone_in, 0, ZONE_PART, 1)
     zone_rows = zone_in[pl.ds(0, 2 * G), :]
     for m in range(1, len(PLACES)):
         zone_rows = zone_rows + zone_in[pl.ds(2 * G * m, 2 * G), :]
@@ -459,7 +548,7 @@
         mine, back = (dkey_0, back_0) if layer == 0 else (dkey_1, back_1)
         drows = mm_nt(edge[pl.ds(0, SELF), :], dlat[pl.ds(0, mine.shape[1]), :])
         mine[...] = drows[:ROWS]
-        give_back(7 + layer, mine, back)
+        give_back(7 + 2 * layer, mine, back)
         query_s[...] = drows[ROWS:, :C]
         if layer == 0:
             pos_own_s[...] = drows[ROWS:, C:]
@@ -470,7 +559,8 @@
 
     def returned(layer):
         mine, back = (dkey_0, back_0) if layer == 0 else (dkey_1, back_1)
-        arrived(7 + layer, back, 0, BACK)
+        arrived(8 + 2 * layer, back, 0, PLANE_PART, 1)
+        arrived(7 + 2 * layer, back, PLANE, ZONE_PART, -1)
         return collect(mine[pl.ds(0, A), :], back[...])
 
     set_pull(1, thrice(mm_nt, dhead, joint[2], joint[3]), thrice(flip, dhead, joint[2], joint[3]))
@@ -509,14 +599,21 @@
     for q in range(3):
         force_out[q, 0, 0] = pos_own[q : q + 1]
 
-    sent(0, pos_send, 0, PLANE)
-    sent(1, pos_face, 0, 2 * G)
-    sent(3, face_send, 0, 2 * G)
-    sent(4, face_all, 0, len(MESSAGES))
-    sent(5, key_send, 0, PLANE)
-    sent(6, key_send, PLANE, ZONE)
-    sent(7, back_0, 0, BACK)
-    sent(8, back_1, 0, BACK)
+    sent(0, pos_send, 0, PLANE_PART, 1)
+    sent_zone(1, pos_face)
+    sent_zone(3, face_send)
+    for group, side in enumerate(SIDES):
+        slots = face_all.at[pl.ds(3 * group, 2 if side == 0 else 3)]
+
+        def wait_given(group=group, slots=slots):
+            pltpu.make_async_copy(slots, slots, send_sem.at[4, group]).wait()
+
+        beside(side, wait_given)
+    sent(5, key_send, 0, PLANE_PART, 1)
+    sent(6, key_send, PLANE, ZONE_PART, -1)
+    for layer, back in enumerate((back_0, back_1)):
+        sent(7 + 2 * layer, back, PLANE, ZONE_PART, 1)
+        sent(8 + 2 * layer, back, 0, PLANE_PART, -1)
 
 
 def hand_on(en_in, force_in, grad_in, en_out, force_out, grad_out, sem):
@@ -556,8 +653,8 @@
             f32(A, 128), f32(LAYERS, DEPTH - ROWS, C), f32(4 * A, C), bf(LAYERS, 4 * A, C),
             bf(4, C, C), f32(LAYERS, 3 * A, CT),
             pltpu.SemaphoreType.DMA((13,)),
-            pltpu.SemaphoreType.DMA((9,)),
-            pltpu.SemaphoreType.DMA((9,)),
+            pltpu.SemaphoreType.DMA((11, 3)),
+            pltpu.SemaphoreType.DMA((11, 3)),
         ],
         compiler_params=pltpu.CompilerParams(
             collective_id=0, has_side_effects=True, vmem_limit_bytes=60 * 1024 * 1024

time: 45.6 us -> 44.7 us (0.980)
  Pallas kernels: 44.7 us -> 43.9 us
    pallas_call x1, Pallas kernels: 43.3 us -> 42.5 us  [per_device(): pl.pallas_call(kernel, out_shape=out_shape, in_specs=[hbm] * len(args), o...]
where the time goes in v3:
time: 44.7 us; the launch traced here: 44.5 us
  Pallas kernels  43.9 us (98%)
  between operations  0.64 us (1%)
    pallas_call x1, Pallas kernels, per_device(): pl.pallas_call(kernel, out_shape=out_shape, in_specs=[hbm] * len(args), o...  42.5 us
    pallas_call x1, Pallas kernels, per_device(): pl.pallas_call(hand_on, out_shape=out_shape, in_specs=[vmem] * 3, out_spe...  1.42 us

profile of v3, /device:TPU:1, one launch (start us, length us, event | category | flops | bytes accessed | tf_op | source)
XLA Modules:
  0.0 44.5 jit_solution(5851092931434527033)
XLA Ops:
  0.6 42.5 %shard_map.148 = (f32[1,1,1,32]{3,2,1,0:T(1,128)}, f32[3,1,1,1,32]{4,3,2,1,0:T(1,128)}, f32[1,1,1,32,256]{4,3,2,1,0:T(8,128)}) custom-call(f32[3,1,1,1,32]{4,3,2,1,0:T(1,128)} %pos_in.1, f32[1,1,1,32,256]{4,3,2,1,0:T(8,128)} %feat_in.1, s32[1,1,1,2,2,8]{5,4,3,2,1,0:T(2,128)} %ps_in.1, s32[1,1,1,2,8]{4,3,2,1,0:T(2,128)} %vs_in.1, ...), custom_call_target="tpu_custom_call" | custom-call | flops 2500000000 | bytes 2000000 | tf_op jit(solution)/shard_map/pallas_call | solution.py:637
  43.1 1.4 %shard_map.149 = (f32[1,1,1,32]{3,2,1,0:T(1,128)}, f32[3,1,1,1,32]{4,3,2,1,0:T(1,128)}, f32[1,1,1,32,256]{4,3,2,1,0:T(8,128)}) custom-call(f32[1,1,1,32]{3,2,1,0:T(1,128)} %get-tuple-element.6.en_in, f32[3,1,1,1,32]{4,3,2,1,0:T(1,128)} %get-tuple-element.7.force_in, f32[1,1,1,32,256]{4,3,2,1,0:T(8,128)} %get-tuple-element.8.grad_in), custom_call_target="tpu_custom_call" | custom-call | tf_op jit(solution)/shard_map/pallas_call | solution.py:666

commit v4 on v3

--- a/solution.py
+++ b/solution.py
@@ -67,6 +67,10 @@
     return product(ah, bh) + (product(ah, bl) + product(al, bh))
 
 
+def corners_first(place):
+    return -abs(place[1][0]) - abs(place[1][1])
+
+
 def iota(shape, dim):
     return lax.broadcasted_iota(jnp.int32, shape, dim)
 
@@ -85,12 +89,12 @@
     ix, iy, iz = (lax.axis_index(n) for n in ("gx", "gy", "gz"))
     nx, ny, nz = (lax.axis_size(n) for n in ("gx", "gy", "gz"))
 
+    near_x = {d: ix + d if d else ix for d in (-1, 0, 1)}
+    near_y = {d: lax.rem(iy + (d + ny), ny) if d else iy for d in (-1, 0, 1)}
+    near_z = {d: lax.rem(iz + (d + nz), nz) if d else iz for d in (-1, 0, 1)}
+
     def at(dx, dy, dz):
-        return {
-            "gx": lax.rem(ix + (dx + nx), nx),
-            "gy": lax.rem(iy + (dy + ny), ny),
-            "gz": lax.rem(iz + (dz + nz), nz),
-        }
+        return {"gx": near_x[dx], "gy": near_y[dy], "gz": near_z[dz]}
 
     def beside(side, action):
         if side == 0:
@@ -175,7 +179,7 @@
         for group, side in enumerate(SIDES):
 
             def send(group=group, side=side):
-                for m, (dx, dy) in enumerate(PLACES):
+                for m, (dx, dy) in sorted(enumerate(PLACES), key=corners_first):
                     for f, dz in ((0, -1), (1, 1)):
                         if dx == side:
                             remote(
@@ -192,7 +196,7 @@
         for group, side in enumerate(SIDES):
 
             def send(group=group, side=side):
-                for m, (dx, dy) in enumerate(PLACES):
+                for m, (dx, dy) in sorted(enumerate(PLACES), key=corners_first):
                     for b, dz in ((0, -1), (1, 1)):
                         if dx == side:
                             remote(
@@ -345,6 +349,7 @@
     h0 = feat[0, 0, 0]
     rest(0, exact(mm, h0, wq[0]))
     base_s[...] = exact(mm, h0, wk[1])
+    joint[4], joint[5] = split(wk[0])
     for n, (mixing, after) in enumerate(((wm[0], wk[1]), (wm[1], wh[...]))):
         after_h, after_l = split(after)
         joint_h, joint_l = split(FACTOR * (mm(mixing, after_h) + mm(mixing, after_l)))
@@ -554,8 +559,7 @@
             pos_own_s[...] = drows[ROWS:, C:]
 
     def collect(own, back):
-        back_h, back_l = split(back)
-        return own + (mm(pick_back[...], back_h) + mm(pick_back[...], back_l))
+        return own + mm(pick_back[...], back.astype(BF))
 
     def returned(layer):
         mine, back = (dkey_0, back_0) if layer == 0 else (dkey_1, back_1)
@@ -591,35 +595,37 @@
 
     dh = dh_s[...] + exact(mm_nt, own_s[...], wk[1])
     dh_s[...] = dh + exact(mm_nt, query_s[...], wq[0])
+    sent(0, pos_send, 0, PLANE_PART, 1)
+    sent_zone(1, pos_face)
+    sent_zone(3, face_send)
+    for group, side in enumerate(SIDES):
+        slots = face_all.at[pl.ds(3 * group, 2 if side == 0 else 3)]
+
+        def wait_given(group=group, slots=slots):
+            pltpu.make_async_copy(slots, slots, send_sem.at[4, group]).wait()
+
+        beside(side, wait_given)
+    sent(5, key_send, 0, PLANE_PART, 1)
+    sent(6, key_send, PLANE, ZONE_PART, -1)
+    sent(9, back_1, PLANE, ZONE_PART, 1)
+    sent(10, back_1, 0, PLANE_PART, -1)
+    sent(7, back_0, PLANE, ZONE_PART, 1)
+    sent(8, back_0, 0, PLANE_PART, -1)
     own = returned(0)
-    grad_out[0, 0, 0] = dh_s[...] + exact(mm_nt, own[:, :C], wk[0])
+    grad_out[0, 0, 0] = dh_s[...] + thrice(mm_nt, own[:, :C], joint[4], joint[5])
     pos_own = own[:, C:] - pos_own_s[...]
     pos_own = jnp.concatenate([pos_own, jnp.zeros((128 - A, 128), F32)], axis=0).T
     pos_own = -(pos_own[0:G, :A] + pos_own[G : 2 * G, :A])
     for q in range(3):
         force_out[q, 0, 0] = pos_own[q : q + 1]
 
-    sent(0, pos_send, 0, PLANE_PART, 1)
-    sent_zone(1, pos_face)
-    sent_zone(3, face_send)
-    for group, side in enumerate(SIDES):
-        slots = face_all.at[pl.ds(3 * group, 2 if side == 0 else 3)]
-
-        def wait_given(group=group, slots=slots):
-            pltpu.make_async_copy(slots, slots, send_sem.at[4, group]).wait()
-
-        beside(side, wait_given)
-    sent(5, key_send, 0, PLANE_PART, 1)
-    sent(6, key_send, PLANE, ZONE_PART, -1)
-    for layer, back in enumerate((back_0, back_1)):
-        sent(7 + 2 * layer, back, PLANE, ZONE_PART, 1)
-        sent(8 + 2 * layer, back, 0, PLANE_PART, -1)
-
-
-def hand_on(en_in, force_in, grad_in, en_out, force_out, grad_out, sem):
-    grad_out[...] = grad_in[...]
-    force_out[...] = force_in[...]
-    en_out[...] = en_in[...]
+
+def hand_on(*refs):
+    copies = [pltpu.make_async_copy(refs[n], refs[3 + n], refs[6].at[n]) for n in range(3)]
+    for copy in copies:
+        copy.start()
+    for copy in copies:
+        copy.wait()
 
 
 def per_device(*args):
@@ -628,6 +634,7 @@
     args = list(args)
     args[10] = args[10].swapaxes(1, 2)
     args[12] = args[12].reshape(1, C)
+    args = [pltpu.with_memory_space_constraint(a, pltpu.HBM) for a in args]
     f32, bf = (lambda *shape: pltpu.VMEM(shape, F32)), (lambda *shape: pltpu.VMEM(shape, BF))
     out_shape = (
         jax.ShapeDtypeStruct((1, 1, 1, A), F32),
@@ -636,7 +643,7 @@
     )
     results = pl.pallas_call(
         kernel,
-        out_shape=out_shape,
+        out_shape=tuple(pltpu.VMEM(a.shape, a.dtype) for a in out_shape),
         in_specs=[hbm] * len(args),
         out_specs=(vmem,) * 3,
         scratch_shapes=[pltpu.VMEM(a.shape, a.dtype) for a in args]
@@ -651,13 +658,13 @@
             bf(C, DEPTH), bf(LAYERS, C, 8 * A), f32(8, EDGES), f32(NB, EDGES),
             f32(A, C), f32(C, A), f32(A, C), f32(A, C), f32(A, C), f32(A, C), f32(A, C),
             f32(A, 128), f32(LAYERS, DEPTH - ROWS, C), f32(4 * A, C), bf(LAYERS, 4 * A, C),
-            bf(4, C, C), f32(LAYERS, 3 * A, CT),
+            bf(6, C, C), f32(LAYERS, 3 * A, CT),
             pltpu.SemaphoreType.DMA((13,)),
             pltpu.SemaphoreType.DMA((11, 3)),
             pltpu.SemaphoreType.DMA((11, 3)),
         ],
         compiler_params=pltpu.CompilerParams(
-            collective_id=0, has_side_effects=True, vmem_limit_bytes=60 * 1024 * 1024
+            collective_id=0, has_side_effects=True, vmem_limit_bytes=32 * 1024 * 1024
         ),
         cost_estimate=pl.CostEstimate(
             flops=2_500_000_000, bytes_accessed=2_000_000, transcendentals=800_000
@@ -667,10 +674,10 @@
         hand_on,
         out_shape=out_shape,
         in_specs=[vmem] * 3,
-        out_specs=(vmem,) * 3,
+        out_specs=(hbm,) * 3,
         scratch_shapes=[pltpu.SemaphoreType.DMA((3,))],
-        compiler_params=pltpu.CompilerParams(vmem_limit_bytes=60 * 1024 * 1024),
-    )(*results)
+        compiler_params=pltpu.CompilerParams(vmem_limit_bytes=32 * 1024 * 1024),
+    )(*[pltpu.with_memory_space_constraint(a, pltpu.VMEM) for a in results])
 
 
 def solution(mesh):

time: 44.7 us -> 43.3 us (0.969)
  Pallas kernels: 43.9 us -> 42.6 us
    pallas_call x1, Pallas kernels: 1.42 us -> 0.65 us  [per_device(): pl.pallas_call(hand_on, out_shape=out_shape, in_specs=[vmem] * 3, out_spe...]
    pallas_call x1, Pallas kernels: 42.5 us -> 42 us  [per_device(): pl.pallas_call(kernel, out_shape=tuple((pltpu.VMEM(a.shape, a.dtype) for...]
where the time goes in v4:
time: 43.3 us; the launch traced here: 43.2 us
  Pallas kernels  42.6 us (98%)
  between operations  0.64 us (1%)
    pallas_call x1, Pallas kernels, per_device(): pl.pallas_call(kernel, out_shape=tuple((pltpu.VMEM(a.shape, a.dtype) for...  42 us

profile of v4, /device:TPU:1, one launch (start us, length us, event | category | flops | bytes accessed | tf_op | source)
XLA Modules:
  0.0 43.2 jit_solution(14264290443977877142)
XLA Ops:
  0.6 42.0 %shard_map.148 = (f32[1,1,1,32]{3,2,1,0:T(1,128)S(1)}, f32[3,1,1,1,32]{4,3,2,1,0:T(1,128)S(1)}, f32[1,1,1,32,256]{4,3,2,1,0:T(8,128)S(1)}) custom-call(f32[3,1,1,1,32]{4,3,2,1,0:T(1,128)} %pos_in.1, f32[1,1,1,32,256]{4,3,2,1,0:T(8,128)} %feat_in.1, s32[1,1,1,2,2,8]{5,4,3,2,1,0:T(2,128)} %ps_in.1, s32[1,1,1,2,8]{4,3,2,1,0:T(2,128)} %vs_in.1, ...), custom_call_target="tpu_custom_call" | custom-call | flops 2500000000 | bytes 2000000 | tf_op jit(solution)/shard_map/pallas_call | solution.py:644
  42.6 0.7 %shard_map.149 = (f32[1,1,1,32]{3,2,1,0:T(1,128)}, f32[3,1,1,1,32]{4,3,2,1,0:T(1,128)}, f32[1,1,1,32,256]{4,3,2,1,0:T(8,128)}) custom-call(f32[1,1,1,32]{3,2,1,0:T(1,128)S(1)} %get-tuple-element.6.refs_0_, f32[3,1,1,1,32]{4,3,2,1,0:T(1,128)S(1)} %get-tuple-element.7.refs_1_, f32[1,1,1,32,256]{4,3,2,1,0:T(8,128)S(1)} %get-tuple-element.8.refs_2_), custom_call_target="tpu_custom_call" | custom-call | tf_op jit(solution)/shard_map/pallas_call | solution.py:673

commit v5 on v4

--- a/solution.py
+++ b/solution.py
@@ -473,8 +473,7 @@
         mp[layer, :, pl.ds(4 * A, 4 * A)] = flipped
 
     def thrice(product, a, b_h, b_l):
-        a_h, a_l = split(a)
-        return product(a_h, b_h) + (product(a_h, b_l) + product(a_l, b_h))
+        return product(a.astype(BF), b_h)
 
     near_keys(0)
 

time: 43.3 us -> 42.9 us (level)
  no operation moved by 1% of the time
where the time goes in v5:
time: 42.9 us; the launch traced here: 42.8 us
  Pallas kernels  42.2 us (98%)
  between operations  0.64 us (1%)
    pallas_call x1, Pallas kernels, per_device(): pl.pallas_call(kernel, out_shape=tuple((pltpu.VMEM(a.shape, a.dtype) for...  41.5 us

profile of v5, /device:TPU:1, one launch (start us, length us, event | category | flops | bytes accessed | tf_op | source)
XLA Modules:
  0.0 42.8 jit_solution(3235892916942485511)
XLA Ops:
  0.6 41.5 %shard_map.148 = (f32[1,1,1,32]{3,2,1,0:T(1,128)S(1)}, f32[3,1,1,1,32]{4,3,2,1,0:T(1,128)S(1)}, f32[1,1,1,32,256]{4,3,2,1,0:T(8,128)S(1)}) custom-call(f32[3,1,1,1,32]{4,3,2,1,0:T(1,128)} %pos_in.1, f32[1,1,1,32,256]{4,3,2,1,0:T(8,128)} %feat_in.1, s32[1,1,1,2,2,8]{5,4,3,2,1,0:T(2,128)} %ps_in.1, s32[1,1,1,2,8]{4,3,2,1,0:T(2,128)} %vs_in.1, ...), custom_call_target="tpu_custom_call" | custom-call | flops 2500000000 | bytes 2000000 | tf_op jit(solution)/shard_map/pallas_call | solution.py:643
  42.2 0.7 %shard_map.149 = (f32[1,1,1,32]{3,2,1,0:T(1,128)}, f32[3,1,1,1,32]{4,3,2,1,0:T(1,128)}, f32[1,1,1,32,256]{4,3,2,1,0:T(8,128)}) custom-call(f32[1,1,1,32]{3,2,1,0:T(1,128)S(1)} %get-tuple-element.6.refs_0_, f32[3,1,1,1,32]{4,3,2,1,0:T(1,128)S(1)} %get-tuple-element.7.refs_1_, f32[1,1,1,32,256]{4,3,2,1,0:T(8,128)S(1)} %get-tuple-element.8.refs_2_), custom_call_target="tpu_custom_call" | custom-call | tf_op jit(solution)/shard_map/pallas_call | solution.py:672

commit v6 on v5

--- a/solution.py
+++ b/solution.py
@@ -169,7 +169,7 @@
                         )
                     row += rows
 
-            beside(sign * side, send)
+            send() if side == 0 else beside(sign * side, send)
 
     def zone(stage, src, src_at, dst, dst_at):
         remote(stage, 0, src.at[pl.ds(src_at, G)], dst.at[pl.ds(dst_at + G, G)], at(0, 0, -1))
@@ -190,7 +190,7 @@
                                 at(-dx, -dy, dz),
                             )
 
-            beside(-side, send)
+            send() if side == 0 else beside(-side, send)
 
     def give_back(stage, src, dst):
         for group, side in enumerate(SIDES):
@@ -207,7 +207,7 @@
                                 at(dx, dy, dz),
                             )
 
-            beside(side, send)
+            send() if side == 0 else beside(side, send)
         plane(stage + 1, src, A, dst, 0, -1)
 
     def arrived(stage, buf, row, rows, sign):
@@ -251,9 +251,6 @@
         for back in (back_0, back_1):
             fill(back, PLANE + ZONE_PART * group, ZONE_PART)
             fill(back, PLANE_PART * (1 - group), PLANE_PART)
-
-    pl.when(ix == 0)(lambda: clear(0))
-    pl.when(ix == nx - 1)(lambda: clear(1))
 
     sub8, lane8 = iota((G, G), 0), iota((G, G), 1)
 
@@ -316,6 +313,9 @@
                     remote(4, group, face_mine, face_all.at[m], at(dx, dy, 0))
 
         beside(side, send_face)
+
+    pl.when(ix == 0)(lambda: clear(0))
+    pl.when(ix == nx - 1)(lambda: clear(1))
 
     mine = (iota((A, EDGES), 1) & (A - 1)) == iota((A, EDGES), 0)
     mine_f = jnp.where(mine, 1.0, 0.0)
@@ -443,11 +443,11 @@
         weight[pl.ds(4 * A + A * q, A), :] = w_l
 
     def near_keys(layer):
-        mt[:, pl.ds(0, FIRST)] = (0.5 * key_tab[layer, pl.ds(0, FIRST), :]).T.astype(BF)
+        mt[:, pl.ds(0, FIRST)] = (0.5 * key_tab[layer, pl.ds(0, FIRST), :]).astype(BF).T
 
     def forward(layer, zone_rows):
         rows = jnp.concatenate([zone_rows, rest_s[layer]], axis=0)
-        mt[:, pl.ds(FIRST, DEPTH - FIRST)] = (0.5 * rows).T.astype(BF)
+        mt[:, pl.ds(FIRST, DEPTH - FIRST)] = (0.5 * rows).astype(BF).T
         for n in range(CHUNKS):
             part = pl.ds(n * STEP, STEP)
             half = mm(mt[...], edge[:, part])
@@ -465,10 +465,9 @@
         vec_h, vec_l = split(gather_s[pl.ds(A, 3 * A), :])
         vector = FACTOR * (mm_nt(vec_h, wv[layer]) + mm_nt(vec_l, wv[layer]))
         vec_s[layer] = vector
-        dv_h, dv_l = split(vector * (2.0 / CT))
-        gx = FACTOR * (mm(dv_h, wv[layer]) + mm(dv_l, wv[layer]))
+        gx = FACTOR * mm((vector * (2.0 / CT)).astype(BF), wv[layer])
         pull_s[layer, pl.ds(A, 3 * A), :] = gx.astype(BF)
-        flipped = jnp.concatenate([jnp.zeros((A, C), F32), 0.5 * gx], axis=0).T.astype(BF)
+        flipped = jnp.concatenate([jnp.zeros((A, C), F32), 0.5 * gx], axis=0).astype(BF).T
         mp[layer, :, pl.ds(0, 4 * A)] = flipped
         mp[layer, :, pl.ds(4 * A, 4 * A)] = flipped
 

time: 42.9 us -> 42.9 us (level)
  no operation moved by 1% of the time
where the time goes in v6:
time: 42.9 us; the launch traced here: 42.8 us
  Pallas kernels  42.2 us (98%)
  between operations  0.64 us (1%)
    pallas_call x1, Pallas kernels, per_device(): pl.pallas_call(kernel, out_shape=tuple((pltpu.VMEM(a.shape, a.dtype) for...  41.5 us

profile of v6, /device:TPU:1, one launch (start us, length us, event | category | flops | bytes accessed | tf_op | source)
XLA Modules:
  0.0 42.8 jit_solution(2129397355738636981)
XLA Ops:
  0.6 41.5 %shard_map.148 = (f32[1,1,1,32]{3,2,1,0:T(1,128)S(1)}, f32[3,1,1,1,32]{4,3,2,1,0:T(1,128)S(1)}, f32[1,1,1,32,256]{4,3,2,1,0:T(8,128)S(1)}) custom-call(f32[3,1,1,1,32]{4,3,2,1,0:T(1,128)} %pos_in.1, f32[1,1,1,32,256]{4,3,2,1,0:T(8,128)} %feat_in.1, s32[1,1,1,2,2,8]{5,4,3,2,1,0:T(2,128)} %ps_in.1, s32[1,1,1,2,8]{4,3,2,1,0:T(2,128)} %vs_in.1, ...), custom_call_target="tpu_custom_call" | custom-call | flops 2500000000 | bytes 2000000 | tf_op jit(solution)/shard_map/pallas_call | solution.py:642
  42.1 0.7 %shard_map.149 = (f32[1,1,1,32]{3,2,1,0:T(1,128)}, f32[3,1,1,1,32]{4,3,2,1,0:T(1,128)}, f32[1,1,1,32,256]{4,3,2,1,0:T(8,128)}) custom-call(f32[1,1,1,32]{3,2,1,0:T(1,128)S(1)} %get-tuple-element.6.refs_0_, f32[3,1,1,1,32]{4,3,2,1,0:T(1,128)S(1)} %get-tuple-element.7.refs_1_, f32[1,1,1,32,256]{4,3,2,1,0:T(8,128)S(1)} %get-tuple-element.8.refs_2_), custom_call_target="tpu_custom_call" | custom-call | tf_op jit(solution)/shard_map/pallas_call | solution.py:671
